TPU v7x, 128 devices: a whole 4x4x4 slice. The times are simulated.
128 devices in a mesh: seq: 16 (over y, z), col: 8 (over x, core).
Axes of the slice: x: 4, y: 4, z: 4, core: 2. Of those that a mesh axis runs over, the one named last changes fastest.
Arguments:
- atom_feats: bfloat16 [16, 16384, 128], P(None, ('seq', 'col')), may hold values from -6 to 6
- atom_pair: bfloat16 [16, 512, 32, 128], P(None, ('seq', 'col'))
- key_shift: int32 [512], P(('seq', 'col')), may hold values from -1 to 1
- atom_token: int32 [16384], P(('seq', 'col')), may hold values from 0 to 2047, as said below
- token_count: int32 [2048], P('seq'), may hold values from 1 to 15, as said below
- atom_gain: float32 [128], replicated, may hold values from 0.5 to 1.5
- atom_qkv: bfloat16 [128, 384], replicated, may hold values from -0.5 to 0.5
- atom_out_proj: bfloat16 [128, 128], replicated, may hold values from -0.5 to 0.5
- atom_pair_proj: bfloat16 [16, 4], replicated
- pool_proj: bfloat16 [128, 768], replicated, may hold values from -0.5 to 0.5
- token_gain: float32 [768], replicated, may hold values from 0.5 to 1.5
- token_qkvg: bfloat16 [768, 4, 768], P(None, None, 'col'), may hold values from -0.21875 to 0.21875
- pair_tiles: bfloat16 [2048, 2048, 128], P('seq', 'col')
- pair_proj: bfloat16 [128, 16], replicated
- token_out_proj: bfloat16 [768, 768], replicated, may hold values from -0.21875 to 0.21875
- return_proj: bfloat16 [768, 128], replicated, may hold values from -0.21875 to 0.21875
Outputs:
- atom_update: bfloat16 [16, 16384, 128], P(None, ('seq', 'col'))
Inputs may be any that keep to these rules, and one draw needn't show every extreme that they name: `token_count`: the tokens of one index of seq, 128 in a row, together own exactly 1024 atoms; the first token of each such block has the most atoms. `atom_token`: never falling; token t owns the token_count[t] atoms that follow those of earlier tokens.
All inputs are finite; a program needn't handle non-finite values.
Results may differ from a plain program's by a relative error of at most 0.015.
Values may be sent and summed in bfloat16 or wider, within the bound.
No kernel may reach another device: no remote copies, remote signals or barrier semaphores. Data moves between devices by JAX's collectives and lax.ppermute only.
A program may use at most 192 MiB of HBM per device.

v0:
```python
import functools

import jax
import jax.numpy as jnp
import numpy as np
from jax import lax
from jax.experimental import pallas as pl
from jax.experimental.pallas import tpu as pltpu
from jax.sharding import PartitionSpec as P

EPSILON = 1e-05
LOG2E = float(np.log2(np.e))
VMEM_LIMIT = 48 * 1024 * 1024
BF = jnp.bfloat16
F32 = jnp.float32


def params(limit=VMEM_LIMIT):
    return pltpu.CompilerParams(dimension_semantics=("arbitrary",), vmem_limit_bytes=limit)


def layer_norm(values, norm_gain):
    centred = values - jnp.mean(values, axis=-1, keepdims=True)
    variance = jnp.mean(centred * centred, axis=-1, keepdims=True)
    return centred * lax.rsqrt(variance + EPSILON) * norm_gain


def dot(a, b, contract):
    return lax.dot_general(a, b, ((contract[0:1], contract[1:2]), ((), ())), preferred_element_type=F32)


def atom_kernel(
    shift_ref, off_ref, wpair_ref, feats_ref, before_ref, after_ref, pair_ref, gain_ref,
    qkv_ref, out_proj_ref, mid_ref, bias_ref, kv_ref, *, limit_atoms,
):
    samples, atoms, channels = feats_ref.shape
    cpair, blocks, qblock, window = pair_ref.shape
    margin = window // 2 - qblock // 2 + qblock
    heads = wpair_ref.shape[1]
    head_dim = channels // heads
    rows = atoms + 2 * margin

    @pl.when(pl.program_id(0) == 0)
    def _():
        lane = lax.broadcasted_iota(jnp.int32, (qblock, window), 1)
        for b in range(blocks):
            tiles = [pair_ref[c, b].astype(F32) for c in range(cpair)]
            key = off_ref[0] - margin + qblock * (b + 1 + shift_ref[b]) + lane
            ok = (key >= 0) & (key < limit_atoms)
            for h in range(heads):
                acc = tiles[0] * wpair_ref[0, h]
                for c in range(1, cpair):
                    acc = acc + tiles[c] * wpair_ref[c, h]
                bias_ref[b, h * qblock : (h + 1) * qblock, :] = jnp.where(ok, acc * LOG2E, -1e9)

    feats = feats_ref[...]
    stacked = jnp.concatenate(
        [before_ref[:, atoms - margin :], feats, after_ref[:, :margin]], axis=1
    )
    flat = stacked.reshape(samples * rows, channels).astype(F32)
    normed = layer_norm(flat, gain_ref[...]).astype(BF)
    projected = jnp.dot(normed, qkv_ref[...], preferred_element_type=F32)
    kv_ref[...] = projected[:, channels:].astype(BF).reshape(samples, rows, 2 * channels)
    scale = LOG2E / float(np.sqrt(head_dim))
    queries = (projected[:, :channels] * scale).astype(BF).reshape(samples, rows, channels)
    lane_head = lax.broadcasted_iota(jnp.int32, (qblock, channels), 1) // head_dim
    masks = [lane_head == h for h in range(heads)]
    ones = jnp.ones((window, channels), BF)
    zero = jnp.zeros((qblock, channels), BF)
    attended = []
    pairs = [(s, b) for s in range(samples) for b in range(blocks)]
    group = 8
    for first in range(0, len(pairs), group):
        part = pairs[first : first + group]
        wins = [
            kv_ref[s, pl.ds(pl.multiple_of(qblock * (b + 1 + shift_ref[b]), qblock), window), :]
            for s, b in part
        ]
        scores = []
        for (s, b), win in zip(part, wins):
            q = queries[s, margin + b * qblock : margin + (b + 1) * qblock, :]
            spread = jnp.concatenate([jnp.where(m, q, zero) for m in masks], axis=0)
            scores.append(dot(spread, win[:, :channels], (1, 1)) + bias_ref[b])
        weights = [jnp.exp2(x - jnp.max(x, axis=1, keepdims=True)).astype(BF) for x in scores]
        for win, x in zip(wins, weights):
            both = jnp.concatenate([win[:, channels:], ones], axis=1)
            mixed = jnp.dot(x, both, preferred_element_type=F32)
            out = mixed[:qblock]
            for h in range(1, heads):
                own = mixed[h * qblock : (h + 1) * qblock]
                out = jnp.where(jnp.concatenate([masks[h], masks[h]], axis=1), own, out)
            attended.append((out[:, :channels] / out[:, channels:]).astype(BF))
    attended = jnp.concatenate(attended, axis=0)
    update = jnp.dot(attended, out_proj_ref[...], preferred_element_type=F32)
    mid = feats.reshape(samples * atoms, channels).astype(F32) + update
    mid_ref[...] = mid.astype(BF).reshape(samples, atoms, channels)


def atom_attention(feats, before, after, pair, shift, offset, limit, gain, qkv, out_proj, wpair):
    samples, atoms, channels = feats.shape
    blocks, qblock, window = pair.shape[1:]
    rows = atoms + 2 * (window // 2 - qblock // 2 + qblock)
    step = 8
    whole = lambda a: pl.BlockSpec(a.shape, lambda i: (0,) * a.ndim)
    part = lambda a: pl.BlockSpec((step,) + a.shape[1:], lambda i: (i, 0, 0))
    smem = pl.BlockSpec(memory_space=pltpu.SMEM)
    return pl.pallas_call(
        functools.partial(atom_kernel, limit_atoms=limit),
        grid=(samples // step,),
        in_specs=[smem, smem, smem, part(feats), part(before), part(after), whole(pair),
                  whole(gain), whole(qkv), whole(out_proj)],
        out_specs=part(feats),
        out_shape=jax.ShapeDtypeStruct(feats.shape, BF),
        scratch_shapes=[
            pltpu.VMEM((blocks, qblock * wpair.shape[1], window), F32),
            pltpu.VMEM((step, rows, 2 * channels), BF),
        ],
        compiler_params=params(),
        cost_estimate=pl.CostEstimate(flops=8_000_000_000, bytes_accessed=3_000_000, transcendentals=1_000_000),
        name="atom_attention",
    )(shift, offset, wpair, feats, before, after, pair, gain, qkv, out_proj)


def tie(value, *others):
    def kernel(*refs):
        pass
    hbm = pl.BlockSpec(memory_space=pl.ANY)
    return pl.pallas_call(
        kernel,
        in_specs=[hbm] * (1 + len(others)),
        out_specs=hbm,
        out_shape=jax.ShapeDtypeStruct(value.shape, value.dtype),
        input_output_aliases={0: 0},
        name="tie",
    )(value, *others)


def tie(value, *others):
    def kernel(*refs):
        pass
    hbm = pl.BlockSpec(memory_space=pl.ANY)
    return pl.pallas_call(
        kernel,
        in_specs=[hbm] * (1 + len(others)),
        out_specs=hbm,
        out_shape=jax.ShapeDtypeStruct(value.shape, value.dtype),
        input_output_aliases={0: 0},
        name="tie",
    )(value, *others)


def split_kernel(value_ref, after_ref, first_ref, rest_ref, sems):
    rows = first_ref.shape[0]
    copies = [
        pltpu.make_async_copy(value_ref.at[pl.ds(0, rows)], first_ref, sems.at[0]),
        pltpu.make_async_copy(value_ref.at[pl.ds(rows, rest_ref.shape[0])], rest_ref, sems.at[1]),
    ]
    for copy in copies:
        copy.start()
    for copy in copies:
        copy.wait()


def split_rows(value, rows, after):
    hbm = pl.BlockSpec(memory_space=pl.ANY)
    total, width = value.shape
    return pl.pallas_call(
        split_kernel,
        in_specs=[pl.BlockSpec(memory_space=pltpu.VMEM), hbm],
        out_specs=[hbm] * 2,
        out_shape=[
            jax.ShapeDtypeStruct((rows, width), value.dtype),
            jax.ShapeDtypeStruct((total - rows, width), value.dtype),
        ],
        scratch_shapes=[pltpu.SemaphoreType.DMA((2,))],
        cost_estimate=pl.CostEstimate(flops=0, bytes_accessed=4 * value.size, transcendentals=0),
        name="split_rows",
    )(value, after)


def token_kernel(
    mid_ref, count_row_ref, count_col_ref, pool_ref, gain_ref, w_hbm, qkv_ref, gate_ref,
    single_ref, normed_ref, w_ref, sem, *, head_dim,
):
    load = pltpu.make_async_copy(w_hbm, w_ref, sem)
    load.start()
    peers, samples, atoms, channels = mid_ref.shape
    toks = count_col_ref.shape[0]
    total = peers * atoms
    counts = count_col_ref[...]
    row = lax.broadcasted_iota(jnp.int32, (toks, toks), 0)
    col = lax.broadcasted_iota(jnp.int32, (toks, toks), 1)
    spread = jnp.broadcast_to(count_row_ref[...], (toks, toks))
    ends = jnp.sum(jnp.where(col <= row, spread, 0.0), axis=1, keepdims=True)
    begins = ends - counts
    atom = lax.broadcasted_iota(jnp.int32, (toks, total), 1).astype(F32)
    onehot = jnp.where((atom >= begins) & (atom < ends), 1.0, 0.0).astype(BF)
    for s in range(samples):
        mid = mid_ref[:, s].reshape(total, channels)
        lifted = jnp.dot(mid, pool_ref[...], preferred_element_type=F32)
        lifted = jnp.maximum(lifted, 0.0).astype(BF)
        single = jnp.dot(onehot, lifted, preferred_element_type=F32) / counts
        single_ref[s] = single
        normed_ref[s * toks : (s + 1) * toks, :] = layer_norm(single, gain_ref[...]).astype(BF)

    load.wait()
    scale = LOG2E / float(np.sqrt(head_dim))
    width = w_ref.shape[1] // 4
    local = width // head_dim
    for p in range(peers):
        turned = dot(w_ref[p], normed_ref[...], (1, 1))
        for hh in range(local):
            for s in range(samples):
                for f in range(4):
                    lo = f * width + hh * head_dim
                    tile = turned[lo : lo + head_dim, s * toks : (s + 1) * toks]
                    if f == 0:
                        tile = tile * scale
                    if f < 3:
                        qkv_ref[p * local + hh, s, f] = tile.astype(BF)
                    else:
                        gate_ref[p * local + hh, s] = tile.astype(BF)


def pool_and_project(mid, count, pool, gain, w, heads):
    peers, samples, atoms, channels = mid.shape
    toks = count.shape[0]
    width = pool.shape[1]
    head_dim = width // heads
    count = count.astype(F32)
    row, col = count.reshape(1, toks), count.reshape(toks, 1)
    gain = gain.reshape(1, width)
    vmem = pl.BlockSpec(memory_space=pltpu.VMEM)
    return pl.pallas_call(
        functools.partial(token_kernel, head_dim=head_dim),
        in_specs=[vmem] * 5 + [pl.BlockSpec(memory_space=pl.ANY)],
        out_specs=[vmem] * 3,
        out_shape=[
            jax.ShapeDtypeStruct((heads, samples, 3, head_dim, toks), BF),
            jax.ShapeDtypeStruct((heads, samples, head_dim, toks), BF),
            jax.ShapeDtypeStruct((samples, toks, width), F32),
        ],
        scratch_shapes=[
            pltpu.VMEM((samples * toks, width), BF),
            pltpu.VMEM(w.shape, BF),
            pltpu.SemaphoreType.DMA,
        ],
        compiler_params=pltpu.CompilerParams(vmem_limit_bytes=VMEM_LIMIT),
        cost_estimate=pl.CostEstimate(flops=6_000_000_000, bytes_accessed=8_000_000, transcendentals=1000),
        name="pool_and_project",
    )(mid, row, col, pool, gain, w)


def attend_kernel(place_ref, qkv_ref, gathered_ref, *refs, gathered_rows):
    pieces, (out_ref, keys_ref, values_ref) = refs[:-3], refs[-3:]
    peers, samples, _, head_dim, toks = qkv_ref.shape
    qblocks = out_ref.shape[0]
    width = gathered_ref.shape[2]
    per = width // toks
    step = pl.program_id(0)
    first = gathered_rows // (qblocks * toks)
    chip, core = place_ref[0], place_ref[1]
    chips = len(pieces) // 2

    def load(order):
        for s in range(samples):
            for i, p in enumerate(order):
                lanes = slice(i * toks, (i + 1) * toks)
                keys_ref[s, :, lanes] = qkv_ref[p, s, 1]
                values_ref[s, :head_dim, lanes] = qkv_ref[p, s, 2]
            values_ref[s, head_dim:, :] = jnp.ones((values_ref.shape[1] - head_dim, peers * toks), BF)

    def attend(tiles):
        for s in range(samples):
            queries = jnp.concatenate(
                [qkv_ref[step * qblocks + j, s, 0] for j in range(qblocks)], axis=1
            ).T
            top = None
            for i, tile in enumerate(tiles):
                lanes = slice(i * width, (i + 1) * width)
                scores = dot(queries, keys_ref[s, :, lanes], (1, 0)) + tile[...].astype(F32)
                peak = jnp.max(scores, axis=1, keepdims=True)
                if i > 0:
                    peak = jnp.maximum(top, peak)
                weights = jnp.exp2(scores - peak).astype(BF)
                part = dot(weights, values_ref[s, :, lanes], (1, 1))
                mixed = part if i == 0 else mixed * jnp.exp2(top - peak) + part
                top = peak
            turned = (mixed / mixed[:, head_dim : head_dim + 1]).T
            for j in range(qblocks):
                out_ref[j, s] = turned[:head_dim, j * toks : (j + 1) * toks].astype(BF)

    @pl.when(step == 0)
    def _():
        load(list(range(peers)))

    @pl.when(step == first)
    def _():
        order = []
        for i in range(2 * chips):
            source = lax.rem(chip + chips - i % chips, chips) * 2 + (core if i < chips else 1 - core)
            order += [source * per + j for j in range(per)]
        load(order)

    @pl.when(step < first)
    def _():
        attend([gathered_ref.at[c] for c in range(gathered_ref.shape[0])])

    @pl.when(step >= first)
    def _():
        attend(pieces)


def token_attention(place, qkv, gathered, pieces):
    peers, samples, _, head_dim, toks = qkv.shape
    cols, rows, width = gathered.shape
    qblocks = 4
    tile = qblocks * toks
    keys = peers * toks
    first = rows // tile
    late = lambda i: (jnp.maximum(i - first, 0), 0)
    return pl.pallas_call(
        functools.partial(attend_kernel, gathered_rows=rows),
        grid=(keys // tile,),
        in_specs=[
            pl.BlockSpec(memory_space=pltpu.SMEM),
            pl.BlockSpec(qkv.shape, lambda i: (0, 0, 0, 0, 0)),
            pl.BlockSpec((cols, tile, width), lambda i: (0, jnp.minimum(i, first - 1), 0)),
        ] + [pl.BlockSpec((tile, width), late)] * len(pieces),
        out_specs=pl.BlockSpec((qblocks, samples, head_dim, toks), lambda i: (i, 0, 0, 0)),
        out_shape=jax.ShapeDtypeStruct((peers, samples, head_dim, toks), BF),
        scratch_shapes=[
            pltpu.VMEM((samples, head_dim, keys), BF),
            pltpu.VMEM((samples, head_dim + 16, keys), BF),
        ],
        compiler_params=params(58 * 1024 * 1024),
        cost_estimate=pl.CostEstimate(
            flops=4 * samples * keys * keys * 128, bytes_accessed=2 * keys * keys + 2 * qkv.size,
            transcendentals=samples * keys * keys,
        ),
        name="token_attention",
    )(place, qkv, gathered, *pieces)


def out_kernel(mixed_ref, gate_ref, single_ref, out_proj_ref, return_ref, back_ref):
    heads, samples, head_dim, toks = mixed_ref.shape
    for s in range(samples):
        gate = jax.nn.sigmoid(gate_ref[:, s].astype(F32))
        gated = (gate * mixed_ref[:, s].astype(F32)).astype(BF).reshape(heads * head_dim, toks)
        new = single_ref[s] + dot(gated, out_proj_ref[...], (0, 0))
        back_ref[s] = jnp.dot(new.astype(BF), return_ref[...], preferred_element_type=F32).astype(BF)


def out_project(mixed, gate, single, out_proj, return_proj):
    return pl.pallas_call(
        out_kernel,
        out_shape=jax.ShapeDtypeStruct(single.shape[:2] + return_proj.shape[1:], BF),
        compiler_params=pltpu.CompilerParams(vmem_limit_bytes=VMEM_LIMIT),
        cost_estimate=pl.CostEstimate(flops=400_000_000, bytes_accessed=4_000_000, transcendentals=200_000),
        name="out_project",
    )(mixed, gate, single, out_proj, return_proj)


def spread_kernel(tok_ref, back_ref, mid_ref, out_ref):
    samples, atoms, channels = mid_ref.shape
    toks = back_ref.shape[1]
    col = lax.broadcasted_iota(jnp.int32, (atoms, toks), 1)
    onehot = jnp.where(col == tok_ref[...], 1.0, 0.0).astype(BF)
    for s in range(samples):
        spread = jnp.dot(onehot, back_ref[s], preferred_element_type=F32)
        out_ref[s] = (mid_ref[s].astype(F32) + spread).astype(BF)


def spread_back(local_tok, back, mid):
    return pl.pallas_call(
        spread_kernel,
        out_shape=jax.ShapeDtypeStruct(mid.shape, BF),
        compiler_params=pltpu.CompilerParams(vmem_limit_bytes=VMEM_LIMIT),
        cost_estimate=pl.CostEstimate(flops=100_000_000, bytes_accessed=2_000_000, transcendentals=0),
        name="spread_back",
    )(local_tok, back, mid)


def shards(
    atom_feats, atom_pair, key_shift, atom_token, token_count, atom_gain, atom_qkv,
    atom_out_proj, atom_pair_proj, pool_proj, token_gain, token_qkvg, pair_tiles, pair_proj,
    token_out_proj, return_proj,
):
    samples, atoms, channels = atom_feats.shape
    toks = token_count.shape[0]
    width = token_qkvg.shape[0]
    heads = pair_proj.shape[1]
    peers = lax.axis_size("col")
    seqs = lax.axis_size("seq")
    devices = peers * seqs
    qblock, window = atom_pair.shape[2:]
    margin = window // 2 - qblock // 2 + qblock

    up = [(i, i + 1) for i in range(devices - 1)]
    down = [(j, i) for i, j in up]
    before = lax.ppermute(atom_feats, ("seq", "col"), up)
    after = lax.ppermute(atom_feats, ("seq", "col"), down)

    turned_w = jnp.transpose(token_qkvg, (1, 2, 0)).reshape(-1, width)
    all_w = lax.all_gather(turned_w, "col", axis=0)

    tile_bias = jnp.einsum("ijc,ch->hij", pair_tiles, pair_proj, preferred_element_type=F32)
    tile_bias = (tile_bias * LOG2E).astype(BF)
    head_bias = lax.all_to_all(tile_bias, "seq", split_axis=0, concat_axis=0, tiled=True)

    index = lax.axis_index(("seq", "col"))
    offset = (index * atoms).astype(jnp.int32).reshape(1)
    mid = atom_attention(
        atom_feats, before, after, atom_pair, key_shift, offset, atoms * devices,
        atom_gain.reshape(1, -1), atom_qkv, atom_out_proj, atom_pair_proj.astype(F32),
    )
    chips = peers // 2
    first, rest = split_rows(head_bias.reshape(seqs * toks, -1), 3 * seqs * toks // 4, mid)
    gathered = lax.all_gather(first, "col", axis=0)

    mine = lax.all_to_all(
        mid.reshape(peers, samples // peers, atoms, channels), "col", split_axis=0, concat_axis=0, tiled=True
    )
    qkv, gate, single = pool_and_project(mine, token_count, pool_proj, token_gain, all_w, heads)
    pieces = [tie(rest, single)]
    for hop in range(1, chips):
        pairs = [(2 * x + k, 2 * ((x + hop) % chips) + k) for x in range(chips) for k in range(2)]
        pieces.append(lax.ppermute(pieces[0], "col", pairs))
    swap = [(i, i ^ 1) for i in range(peers)]
    pieces += [lax.ppermute(piece, "col", swap) for piece in pieces]
    qkv = lax.all_to_all(qkv, "seq", split_axis=0, concat_axis=0, tiled=True)
    col = lax.axis_index("col")
    place = jnp.stack([col // 2, col % 2]).astype(jnp.int32)
    mixed = token_attention(place, qkv, gathered, pieces)
    mixed = lax.all_to_all(mixed, "seq", split_axis=0, concat_axis=0, tiled=True)
    back = out_project(mixed, gate, single, token_out_proj, return_proj)
    back = lax.all_gather(back, "col", axis=0, tiled=True)
    local_tok = (atom_token - lax.axis_index("seq") * toks).reshape(atoms, 1)
    return spread_back(local_tok, back, mid)


def solution(mesh):
    placed = (
        P(None, ("seq", "col"), None),
        P(None, ("seq", "col"), None, None),
        P(("seq", "col")),
        P(("seq", "col")),
        P("seq"),
        P(),
        P(),
        P(),
        P(),
        P(),
        P(),
        P(None, None, "col"),
        P("seq", "col", None),
        P(),
        P(),
        P(),
    )
    return jax.shard_map(
        shards, mesh=mesh, in_specs=placed, out_specs=P(None, ("seq", "col"), None), check_vma=False
    )
```

profile of v0, /device:TPU:1, one launch (start us, length us, event | category | flops | bytes accessed | tf_op | source)
XLA Modules:
  0.0 156.1 jit_solution(18174396409661863360)
XLA Ops:
  6.5 0.7 all-gather.4.cloned.1.call-update
  7.3 4.6 %collective-permute-start = (bf16[16,128,128]{2,1,0:T(8,128)(2,1)}, bf16[16,128,128]{2,1,0:T(8,128)(2,1)S(1)}, u32[]{:S(2)}, u32[]{:S(2)}) collective-permute-start(bf16[16,128,128]{2,1,0:T(8,128)(2,1)} %feats_ref.1), channel_id=1, source_target_pairs={{0,1},{1,2},{2,3},{3,4},{4,5},{5,6},{6,7},{7,8},{8,9},{9,10},{10,1... | collective-permute-start | bytes 1572872 | tf_op jit(solution)/shard_map/ppermute | solution.py:401
  12.0 1.9 %collective-permute-start.1 = (bf16[16,128,128]{2,1,0:T(8,128)(2,1)}, bf16[16,128,128]{2,1,0:T(8,128)(2,1)S(1)}, u32[]{:S(2)}, u32[]{:S(2)}) collective-permute-start(bf16[16,128,128]{2,1,0:T(8,128)(2,1)} %feats_ref.1), channel_id=1, source_target_pairs={{1,0},{2,1},{3,2},{4,3},{5,4},{6,5},{7,6},{8,7},{9,8},{10,9},{11,1... | collective-permute-start | bytes 1572872 | tf_op jit(solution)/shard_map/ppermute | solution.py:402
  13.9 5.7 %multiply_convert_fusion = bf16[16,128,256]{2,0,1:T(8,128)(2,1)S(1)} fusion(bf16[128,256,128]{2,1,0:T(8,128)(2,1)} %param.28, bf16[128,16]{0,1:T(8,128)(2,1)S(1)} %copy-done), kind=kOutput, calls=%fused_computation | convolution fusion | flops 135266304 | bytes 9441280 | tf_op jit(solution)/shard_map/ijc,ch->hij/dot_general | solution.py:407
  19.6 1.3 copy.28
  20.9 7.8 %all-to-all-start.2 = ((bf16[16,128,256]{2,1,0:T(8,128)(2,1)}), bf16[16,128,256]{2,1,0:T(8,128)(2,1)}, u32[]{:S(2)}, u32[]{:S(2)}) async-start(bf16[16,128,256]{2,1,0:T(8,128)(2,1)} %copy.28), calls=%async_computation.2 | async-start | bytes 2097152 | tf_op jit(solution)/shard_map/all_to_all | solution.py:409
  29.0 7.3 %atom_attention.1.after_ref.mid_ref = bf16[16,128,128]{2,1,0:T(8,128)(2,1)S(1)} custom-call(s32[4]{0:T(128)S(1)} %copy-done.12, s32[1]{0:T(128)} %bitcast.3.off_ref, f32[16,4]{1,0:T(8,128)S(1)} %copy.26.wpair_ref, bf16[16,128,128]{2,1,0:T(8,128)(2,1)S(1)} %copy-done.7, bf16[16,128,128]{2,1,0:T(8,128)(2,1)S(1)} %collective-permute-done.before_ref, ...), custom_call_target="tpu_custom_call" | custom-call | flops 8000000000 | bytes 3000000 | tf_op jit(solution)/shard_map/atom_attention/pallas_call | solution.py:107
  36.3 0.8 copy-done.1
  37.1 6.0 %all-to-all-done.2 = bf16[16,128,256]{2,1,0:T(8,128)(2,1)} async-done(((bf16[16,128,256]{2,1,0:T(8,128)(2,1)}), bf16[16,128,256]{2,1,0:T(8,128)(2,1)}, u32[]{:S(2)}, u32[]{:S(2)}) %all-to-all-start.2) | async-done | bytes 1048608 | tf_op jit(solution)/shard_map/all_to_all | solution.py:409
  43.1 2.3 %split_rows.1 = (bf16[1536,256]{1,0:T(8,128)(2,1)}, bf16[512,256]{1,0:T(8,128)(2,1)}) custom-call(bf16[2048,256]{1,0:T(8,128)(2,1)} %bitcast.11.value_ref, bf16[16,128,128]{2,1,0:T(8,128)(2,1)} %copy-done.1), custom_call_target="tpu_custom_call" | custom-call | bytes 2097152 | tf_op jit(solution)/shard_map/split_rows/pallas_call | solution.py:167
  45.4 8.2 %all-to-all-start = ((bf16[8,2,128,128]{3,2,1,0:T(8,128)(2,1)}), bf16[8,2,128,128]{3,2,1,0:T(8,128)(2,1)S(1)}, u32[]{:S(2)}, u32[]{:S(2)}) async-start(bf16[8,2,128,128]{3,2,1,0:T(8,128)(2,1)} %bitcast.20), calls=%async_computation | async-start | bytes 1048576 | tf_op jit(solution)/shard_map/all_to_all | solution.py:421
  53.8 9.6 %all-to-all-done.mid_ref = bf16[8,2,128,128]{3,2,1,0:T(8,128)(2,1)S(1)} async-done(((bf16[8,2,128,128]{3,2,1,0:T(8,128)(2,1)}), bf16[8,2,128,128]{3,2,1,0:T(8,128)(2,1)S(1)}, u32[]{:S(2)}, u32[]{:S(2)}) %all-to-all-start) | async-done | bytes 524320 | tf_op jit(solution)/shard_map/all_to_all | solution.py:421
  63.4 6.4 %pool_and_project.1 = (bf16[16,2,3,48,128]{4,3,2,1,0:T(8,128)(2,1)}, bf16[16,2,48,128]{3,2,1,0:T(8,128)(2,1)S(1)}, f32[2,128,768]{2,1,0:T(8,128)S(1)}) custom-call(bf16[8,2,128,128]{3,2,1,0:T(8,128)(2,1)S(1)} %all-to-all-done.mid_ref, f32[1,128]{1,0:T(1,128)S(1)} %get-tuple-element.16.count_row_ref, f32[128,1]{1,0:T(8,128)S(1)} %copy.27.count_col_ref, ...), custom_call_target="tpu_custom_call" | custom-call | flops 6000000000 | bytes 8000000 | tf_op jit(solution)/shard_map/pool_and_project/pallas_call | solution.py:234
  69.9 0.9 copy-done.3
  70.8 3.7 %all-to-all-start.1 = ((bf16[16,2,3,48,128]{4,3,2,1,0:T(8,128)(2,1)}), bf16[16,2,3,48,128]{4,3,2,1,0:T(8,128)(2,1)S(1)}, u32[]{:S(2)}, u32[]{:S(2)}) async-start(bf16[16,2,3,48,128]{4,3,2,1,0:T(8,128)(2,1)} %get-tuple-element.10), calls=%async_computation.1 | async-start | bytes 2359296 | tf_op jit(solution)/shard_map/all_to_all | solution.py:431
  74.5 0.6 collective-permute-start.4
  75.2 1.1 collective-permute-start.3
  76.3 2.3 %collective-permute-start.5 = (bf16[512,256]{1,0:T(8,128)(2,1)}, bf16[512,256]{1,0:T(8,128)(2,1)S(1)}, u32[]{:S(2)}, u32[]{:S(2)}) collective-permute-start(bf16[512,256]{1,0:T(8,128)(2,1)} %tie.1.refs_0_), channel_id=1, source_target_pairs={{0,1},{1,0},{2,3},{3,2},{4,5},{5,4},{6,7},{7,6},{8,9},{9,8},{10,11... | collective-permute-start | bytes 786440 | tf_op jit(solution)/shard_map/ppermute | solution.py:430
  78.6 9.5 %collective-permute-done.4.refs_3_ = bf16[512,256]{1,0:T(8,128)(2,1)S(1)} collective-permute-done((bf16[512,256]{1,0:T(8,128)(2,1)}, bf16[512,256]{1,0:T(8,128)(2,1)S(1)}, u32[]{:S(2)}, u32[]{:S(2)}) %collective-permute-start.4) | collective-permute-done | bytes 262176 | tf_op jit(solution)/shard_map/ppermute | solution.py:428
  88.1 3.3 %collective-permute-start.8 = (bf16[512,256]{1,0:T(8,128)(2,1)S(1)}, bf16[512,256]{1,0:T(8,128)(2,1)S(1)}, u32[]{:S(2)}, u32[]{:S(2)}) collective-permute-start(bf16[512,256]{1,0:T(8,128)(2,1)S(1)} %collective-permute-done.4.refs_3_), channel_id=1, source_target_pairs={{0,1},{1,0},{2,3},{3,2},{4,5},{5,4},{6,7},{7,6},{8,9},{9,8},{10,11... | collective-permute-start | bytes 786440 | tf_op jit(solution)/shard_map/ppermute | solution.py:430
  91.4 2.2 %collective-permute-start.7 = (bf16[512,256]{1,0:T(8,128)(2,1)S(1)}, bf16[512,256]{1,0:T(8,128)(2,1)S(1)}, u32[]{:S(2)}, u32[]{:S(2)}) collective-permute-start(bf16[512,256]{1,0:T(8,128)(2,1)S(1)} %collective-permute-done.3.refs_2_), channel_id=1, source_target_pairs={{0,1},{1,0},{2,3},{3,2},{4,5},{5,4},{6,7},{7,6},{8,9},{9,8},{10,11... | collective-permute-start | bytes 786440 | tf_op jit(solution)/shard_map/ppermute | solution.py:430
  93.6 3.0 %collective-permute-done.2.refs_1_ = bf16[512,256]{1,0:T(8,128)(2,1)S(1)} collective-permute-done((bf16[512,256]{1,0:T(8,128)(2,1)}, bf16[512,256]{1,0:T(8,128)(2,1)S(1)}, u32[]{:S(2)}, u32[]{:S(2)}) %collective-permute-start.2) | collective-permute-done | bytes 262176 | tf_op jit(solution)/shard_map/ppermute | solution.py:428
  96.5 1.9 %collective-permute-start.6 = (bf16[512,256]{1,0:T(8,128)(2,1)S(1)}, bf16[512,256]{1,0:T(8,128)(2,1)}, u32[]{:S(2)}, u32[]{:S(2)}) collective-permute-start(bf16[512,256]{1,0:T(8,128)(2,1)S(1)} %collective-permute-done.2.refs_1_), channel_id=1, source_target_pairs={{0,1},{1,0},{2,3},{3,2},{4,5},{5,4},{6,7},{7,6},{8,9},{9,8},{10,11... | collective-permute-start | bytes 786440 | tf_op jit(solution)/shard_map/ppermute | solution.py:430
  98.4 0.6 pad_add_fusion.place_ref
  99.1 0.9 collective-permute-done.6.refs_5_
  99.9 2.1 %all-gather.6.cloned.1.call-done = bf16[12288,256]{1,0:T(8,128)(2,1)} async-done(((bf16[1536,256]{1,0:T(8,128)(2,1)}), bf16[12288,256]{1,0:T(8,128)(2,1)}) %all-gather.6.cloned.1.call-update) | async-done | bytes 6291472 | tf_op jit(solution)/shard_map/all_gather | solution.py:419
  102.1 15.7 %token_attention.1 = bf16[16,2,48,128]{3,2,1,0:T(8,128)(2,1)} custom-call(s32[2]{0:T(128)} %pad_add_fusion.place_ref, bf16[16,2,3,48,128]{4,3,2,1,0:T(8,128)(2,1)} %copy-done.14, bf16[8,1536,256]{2,1,0:T(8,128)(2,1)} %bitcast.23, bf16[512,256]{1,0:T(8,128)(2,1)} %tie.1.refs_0_, bf16[512,256]{1,0:T(8,128)(2,1)} %copy-done.19, bf16[512,256]{1,0:T(8,128)(2,1)} %copy-done.18, ...), custom_call_target="tpu_custom_call" | custom-call | flops 4294967296 | bytes 9568256 | tf_op jit(solution)/shard_map/token_attention/pallas_call | solution.py:322
  117.9 5.6 %all-to-all-start.3 = ((bf16[16,2,48,128]{3,2,1,0:T(8,128)(2,1)}), bf16[16,2,48,128]{3,2,1,0:T(8,128)(2,1)S(1)}, u32[]{:S(2)}, u32[]{:S(2)}) async-start(bf16[16,2,48,128]{3,2,1,0:T(8,128)(2,1)} %token_attention.1), calls=%async_computation.3 | async-start | bytes 786432 | tf_op jit(solution)/shard_map/all_to_all | solution.py:435
  123.6 9.1 %all-to-all-done.3.mixed_ref = bf16[16,2,48,128]{3,2,1,0:T(8,128)(2,1)S(1)} async-done(((bf16[16,2,48,128]{3,2,1,0:T(8,128)(2,1)}), bf16[16,2,48,128]{3,2,1,0:T(8,128)(2,1)S(1)}, u32[]{:S(2)}, u32[]{:S(2)}) %all-to-all-start.3) | async-done | bytes 393248 | tf_op jit(solution)/shard_map/all_to_all | solution.py:435
  132.8 0.8 out_project.1
  133.6 14.5 %all_gather.15.back_ref = bf16[16,128,128]{2,1,0:T(8,128)(2,1)S(1)} all-gather(bf16[2,128,128]{2,1,0:T(8,128)(2,1)S(1)} %out_project.1), channel_id=1, replica_groups=mesh['seq'=16,'col'=8] {'col'}, dimensions={0}, use_global_device_ids=true | all-gather | bytes 589824 | tf_op jit(solution)/shard_map/all_gather | solution.py:437
  148.1 1.1 spread_back.1
  (67 shorter events, 0.5 us)
Async XLA Ops:
  6.5 56.9 %all-gather.4.cloned.1.call-start = ((), (), s32[]{:S(2)}) async-start(), calls=%async_computation.4 | async-start | bytes 5308416 | tf_op jit(solution)/shard_map/all_gather | solution.py:405
  7.3 21.6 %copy-start.16 = (bf16[16,4]{0,1:T(4,128)(2,1)S(1)}, bf16[16,4]{0,1:T(4,128)(2,1)}, u32[]{:S(2)}) copy-start(bf16[16,4]{0,1:T(4,128)(2,1)} %param.24) | copy-start | bytes 388
  7.3 21.7 %copy-start.7 = (bf16[16,128,128]{2,1,0:T(8,128)(2,1)S(1)}, bf16[16,128,128]{2,1,0:T(8,128)(2,1)}, u32[]{:S(2)}) copy-start(bf16[16,128,128]{2,1,0:T(8,128)(2,1)} %feats_ref.1) | copy-start | bytes 1572868
  7.3 21.6 %copy-start.8 = (bf16[16,4,32,128]{3,2,1,0:T(8,128)(2,1)S(1)}, bf16[16,4,32,128]{3,2,1,0:T(8,128)(2,1)}, u32[]{:S(2)}) copy-start(bf16[16,4,32,128]{3,2,1,0:T(8,128)(2,1)} %pair_ref.1) | copy-start | bytes 1572868
  7.3 21.6 %copy-start.10 = (bf16[128,384]{1,0:T(8,128)(2,1)S(1)}, bf16[128,384]{1,0:T(8,128)(2,1)}, u32[]{:S(2)}) copy-start(bf16[128,384]{1,0:T(8,128)(2,1)} %qkv_ref.1) | copy-start | bytes 294916
  7.3 21.6 %copy-start.11 = (bf16[128,128]{1,0:T(8,128)(2,1)S(1)}, bf16[128,128]{1,0:T(8,128)(2,1)}, u32[]{:S(2)}) copy-start(bf16[128,128]{1,0:T(8,128)(2,1)} %out_proj_ref.2) | copy-start | bytes 98308
  7.3 21.6 %copy-start.12 = (s32[4]{0:T(128)S(1)}, s32[4]{0:T(128)}, u32[]{:S(2)}) copy-start(s32[4]{0:T(128)} %shift_ref.1) | copy-start | bytes 52
  7.3 21.6 %copy-start.13 = (f32[128]{0:T(128)S(1)}, f32[128]{0:T(128)}, u32[]{:S(2)}) copy-start(f32[128]{0:T(128)} %param.21) | copy-start | bytes 1540
  7.3 21.6 %collective-permute-start = (bf16[16,128,128]{2,1,0:T(8,128)(2,1)}, bf16[16,128,128]{2,1,0:T(8,128)(2,1)S(1)}, u32[]{:S(2)}, u32[]{:S(2)}) collective-permute-start(bf16[16,128,128]{2,1,0:T(8,128)(2,1)} %feats_ref.1), channel_id=1, source_target_pairs={{0,1},{1,2},{2,3},{3,4},{4,5},{5,6},{6,7},{7,8},{8,9},{9,10},{10,1... | collective-permute-start | bytes 1572872 | tf_op jit(solution)/shard_map/ppermute | solution.py:401
  12.0 16.9 %collective-permute-start.1 = (bf16[16,128,128]{2,1,0:T(8,128)(2,1)}, bf16[16,128,128]{2,1,0:T(8,128)(2,1)S(1)}, u32[]{:S(2)}, u32[]{:S(2)}) collective-permute-start(bf16[16,128,128]{2,1,0:T(8,128)(2,1)} %feats_ref.1), channel_id=1, source_target_pairs={{1,0},{2,1},{3,2},{4,3},{5,4},{6,5},{7,6},{8,7},{9,8},{10,9},{11,1... | collective-permute-start | bytes 1572872 | tf_op jit(solution)/shard_map/ppermute | solution.py:402
  20.9 22.2 %all-to-all-start.2 = ((bf16[16,128,256]{2,1,0:T(8,128)(2,1)}), bf16[16,128,256]{2,1,0:T(8,128)(2,1)}, u32[]{:S(2)}, u32[]{:S(2)}) async-start(bf16[16,128,256]{2,1,0:T(8,128)(2,1)} %copy.28), calls=%async_computation.2 | async-start | bytes 2097152 | tf_op jit(solution)/shard_map/all_to_all | solution.py:409
  28.8 73.3 %all-gather.6.cloned.1.call-start = ((), (), s32[]{:S(2)}) async-start(), calls=%async_computation.5 | async-start | bytes 7077888 | tf_op jit(solution)/shard_map/all_gather | solution.py:419
  29.0 24.7 %copy-start.15 = (f32[768]{0:T(1024)S(1)}, f32[768]{0:T(1024)}, u32[]{:S(2)}) copy-start(f32[768]{0:T(1024)} %param.26) | copy-start | bytes 9220
  29.0 24.7 %copy-start.23 = (s32[128]{0:T(128)S(1)}, s32[128]{0:T(128)}, u32[]{:S(2)}) copy-start(s32[128]{0:T(128)} %param.20) | copy-start | bytes 1540
  29.0 34.4 %copy-start.9 = (bf16[128,768]{1,0:T(8,128)(2,1)S(1)}, bf16[128,768]{1,0:T(8,128)(2,1)}, u32[]{:S(2)}) copy-start(bf16[128,768]{1,0:T(8,128)(2,1)} %pool_ref.1) | copy-start | bytes 589828
  45.4 18.0 %all-to-all-start = ((bf16[8,2,128,128]{3,2,1,0:T(8,128)(2,1)}), bf16[8,2,128,128]{3,2,1,0:T(8,128)(2,1)S(1)}, u32[]{:S(2)}, u32[]{:S(2)}) async-start(bf16[8,2,128,128]{3,2,1,0:T(8,128)(2,1)} %bitcast.20), calls=%async_computation | async-start | bytes 1048576 | tf_op jit(solution)/shard_map/all_to_all | solution.py:421
  70.8 29.1 %all-to-all-start.1 = ((bf16[16,2,3,48,128]{4,3,2,1,0:T(8,128)(2,1)}), bf16[16,2,3,48,128]{4,3,2,1,0:T(8,128)(2,1)S(1)}, u32[]{:S(2)}, u32[]{:S(2)}) async-start(bf16[16,2,3,48,128]{4,3,2,1,0:T(8,128)(2,1)} %get-tuple-element.10), calls=%async_computation.1 | async-start | bytes 2359296 | tf_op jit(solution)/shard_map/all_to_all | solution.py:431
  74.5 13.6 %collective-permute-start.4 = (bf16[512,256]{1,0:T(8,128)(2,1)}, bf16[512,256]{1,0:T(8,128)(2,1)S(1)}, u32[]{:S(2)}, u32[]{:S(2)}) collective-permute-start(bf16[512,256]{1,0:T(8,128)(2,1)} %tie.1.refs_0_), channel_id=1, source_target_pairs={{0,6},{1,7},{2,0},{3,1},{4,2},{5,3},{6,4},{7,5},{8,14},{9,15},{10,... | collective-permute-start | bytes 786440 | tf_op jit(solution)/shard_map/ppermute | solution.py:428
  75.2 16.2 %collective-permute-start.3 = (bf16[512,256]{1,0:T(8,128)(2,1)}, bf16[512,256]{1,0:T(8,128)(2,1)S(1)}, u32[]{:S(2)}, u32[]{:S(2)}) collective-permute-start(bf16[512,256]{1,0:T(8,128)(2,1)} %tie.1.refs_0_), channel_id=1, source_target_pairs={{0,4},{1,5},{2,6},{3,7},{4,0},{5,1},{6,2},{7,3},{8,12},{9,13},{10,... | collective-permute-start | bytes 786440 | tf_op jit(solution)/shard_map/ppermute | solution.py:428
  76.3 20.2 %collective-permute-start.2 = (bf16[512,256]{1,0:T(8,128)(2,1)}, bf16[512,256]{1,0:T(8,128)(2,1)S(1)}, u32[]{:S(2)}, u32[]{:S(2)}) collective-permute-start(bf16[512,256]{1,0:T(8,128)(2,1)} %tie.1.refs_0_), channel_id=1, source_target_pairs={{0,2},{1,3},{2,4},{3,5},{4,6},{5,7},{6,0},{7,1},{8,10},{9,11},{10,... | collective-permute-start | bytes 786440 | tf_op jit(solution)/shard_map/ppermute | solution.py:428
  76.3 22.7 %collective-permute-start.5 = (bf16[512,256]{1,0:T(8,128)(2,1)}, bf16[512,256]{1,0:T(8,128)(2,1)S(1)}, u32[]{:S(2)}, u32[]{:S(2)}) collective-permute-start(bf16[512,256]{1,0:T(8,128)(2,1)} %tie.1.refs_0_), channel_id=1, source_target_pairs={{0,1},{1,0},{2,3},{3,2},{4,5},{5,4},{6,7},{7,6},{8,9},{9,8},{10,11... | collective-permute-start | bytes 786440 | tf_op jit(solution)/shard_map/ppermute | solution.py:430
  88.1 14.0 %copy-start.17 = (bf16[512,256]{1,0:T(8,128)(2,1)}, bf16[512,256]{1,0:T(8,128)(2,1)S(1)}, u32[]{:S(2)}) copy-start(bf16[512,256]{1,0:T(8,128)(2,1)S(1)} %collective-permute-done.4.refs_3_) | copy-start | bytes 786436
  88.1 10.9 %collective-permute-start.8 = (bf16[512,256]{1,0:T(8,128)(2,1)S(1)}, bf16[512,256]{1,0:T(8,128)(2,1)S(1)}, u32[]{:S(2)}, u32[]{:S(2)}) collective-permute-start(bf16[512,256]{1,0:T(8,128)(2,1)S(1)} %collective-permute-done.4.refs_3_), channel_id=1, source_target_pairs={{0,1},{1,0},{2,3},{3,2},{4,5},{5,4},{6,7},{7,6},{8,9},{9,8},{10,11... | collective-permute-start | bytes 786440 | tf_op jit(solution)/shard_map/ppermute | solution.py:430
  91.4 10.7 %copy-start.18 = (bf16[512,256]{1,0:T(8,128)(2,1)}, bf16[512,256]{1,0:T(8,128)(2,1)S(1)}, u32[]{:S(2)}) copy-start(bf16[512,256]{1,0:T(8,128)(2,1)S(1)} %collective-permute-done.3.refs_2_) | copy-start | bytes 786436
  91.4 7.7 %collective-permute-start.7 = (bf16[512,256]{1,0:T(8,128)(2,1)S(1)}, bf16[512,256]{1,0:T(8,128)(2,1)S(1)}, u32[]{:S(2)}, u32[]{:S(2)}) collective-permute-start(bf16[512,256]{1,0:T(8,128)(2,1)S(1)} %collective-permute-done.3.refs_2_), channel_id=1, source_target_pairs={{0,1},{1,0},{2,3},{3,2},{4,5},{5,4},{6,7},{7,6},{8,9},{9,8},{10,11... | collective-permute-start | bytes 786440 | tf_op jit(solution)/shard_map/ppermute | solution.py:430
  96.5 3.4 %collective-permute-start.6 = (bf16[512,256]{1,0:T(8,128)(2,1)S(1)}, bf16[512,256]{1,0:T(8,128)(2,1)}, u32[]{:S(2)}, u32[]{:S(2)}) collective-permute-start(bf16[512,256]{1,0:T(8,128)(2,1)S(1)} %collective-permute-done.2.refs_1_), channel_id=1, source_target_pairs={{0,1},{1,0},{2,3},{3,2},{4,5},{5,4},{6,7},{7,6},{8,9},{9,8},{10,11... | collective-permute-start | bytes 786440 | tf_op jit(solution)/shard_map/ppermute | solution.py:430
  102.1 21.5 %copy-start.24 = (s32[128]{0:T(128)S(1)}, s32[128]{0:T(128)}, u32[]{:S(2)}) copy-start(s32[128]{0:T(128)} %param.19) | copy-start | bytes 1540
  102.1 30.7 %copy-start.4 = (f32[2,128,768]{2,1,0:T(8,128)S(1)}, f32[2,128,768]{2,1,0:T(8,128)}, u32[]{:S(2)}) copy-start(f32[2,128,768]{2,1,0:T(8,128)} %copy-done.3) | copy-start | bytes 2359300
  102.1 30.7 %copy-start.5 = (bf16[768,768]{1,0:T(8,128)(2,1)S(1)}, bf16[768,768]{1,0:T(8,128)(2,1)}, u32[]{:S(2)}) copy-start(bf16[768,768]{1,0:T(8,128)(2,1)} %out_proj_ref.3) | copy-start | bytes 3538948
  102.1 30.7 %copy-start.6 = (bf16[768,128]{1,0:T(8,128)(2,1)S(1)}, bf16[768,128]{1,0:T(8,128)(2,1)}, u32[]{:S(2)}) copy-start(bf16[768,128]{1,0:T(8,128)(2,1)} %return_ref.1) | copy-start | bytes 589828
  117.9 30.2 %copy-start.2 = (bf16[16,128,128]{2,1,0:T(8,128)(2,1)S(1)}, bf16[16,128,128]{2,1,0:T(8,128)(2,1)}, u32[]{:S(2)}) copy-start(bf16[16,128,128]{2,1,0:T(8,128)(2,1)} %copy-done.1) | copy-start | bytes 1572868
  117.9 14.9 %all-to-all-start.3 = ((bf16[16,2,48,128]{3,2,1,0:T(8,128)(2,1)}), bf16[16,2,48,128]{3,2,1,0:T(8,128)(2,1)S(1)}, u32[]{:S(2)}, u32[]{:S(2)}) async-start(bf16[16,2,48,128]{3,2,1,0:T(8,128)(2,1)} %token_attention.1), calls=%async_computation.3 | async-start | bytes 786432 | tf_op jit(solution)/shard_map/all_to_all | solution.py:435
  (8 other events, 25.7 us)
Sparse Core Ops, SparseCore 0:
  9.0 37.8 all-gather.3
  48.7 53.3 all-gather.5
where the time goes:
time: 157 us; the launch traced here: 156 us
  starting transfers between devices  43.4 us (28%)
  waiting for transfers between devices  41 us (26%)
  Pallas kernels  33.6 us (21%)
  blocking collectives  14.5 us (9%)
  between operations  13.8 us (9%)
  matrix products  5.66 us (4%)
  local copies, waits for them, and re-layouts  3.51 us (2%)
    pallas_call x1, Pallas kernels, token_attention(): pl.pallas_call(functools.partial(attend_kernel, gathered_rows=rows), grid...  15.7 us
    all_gather x1, blocking collectives, shards(): back = lax.all_gather(back, 'col', axis=0, tiled=True)  14.5 us
    ppermute x3, waiting for transfers between devices, shards(): pieces.append(lax.ppermute(pieces[0], 'col', pairs))  12.5 us
    all_to_all x1, waiting for transfers between devices, shards(): lax.all_to_all(mid.reshape(peers, samples // peers, atoms, channels), 'co...  9.64 us
    ppermute x4, starting transfers between devices, shards(): pieces += [lax.ppermute(piece, 'col', swap) for piece in pieces]  9.61 us
    all_to_all x1, waiting for transfers between devices, shards(): lax.all_to_all(mixed, 'seq', split_axis=0, concat_axis=0, tiled=True)  9.14 us
    all_to_all x1, starting transfers between devices, shards(): lax.all_to_all(mid.reshape(peers, samples // peers, atoms, channels), 'co...  8.22 us
    all_to_all x1, starting transfers between devices, shards(): lax.all_to_all(tile_bias, 'seq', split_axis=0, concat_axis=0, tiled=True)  7.82 us
  transfers between devices with their start and end apart: 15, of which 7 were waited for; matrix products, arithmetic and copies ran while one was open for 5% of the time, Pallas kernels for 10%

commit v1 on v0

--- a/solution.py
+++ b/solution.py
@@ -11,6 +11,7 @@
 EPSILON = 1e-05
 LOG2E = float(np.log2(np.e))
 VMEM_LIMIT = 48 * 1024 * 1024
+VMEM_MOST = 60 * 1024 * 1024
 BF = jnp.bfloat16
 F32 = jnp.float32
 
@@ -31,8 +32,10 @@
 
 def atom_kernel(
     shift_ref, off_ref, wpair_ref, feats_ref, before_ref, after_ref, pair_ref, gain_ref,
-    qkv_ref, out_proj_ref, mid_ref, bias_ref, kv_ref, *, limit_atoms,
+    qkv_ref, out_proj_ref, *refs, limit_atoms,
 ):
+    mid_ref, done_ref, bias_ref, kv_ref = refs[-4:]
+    done_ref[...] = jnp.zeros_like(done_ref)
     samples, atoms, channels = feats_ref.shape
     cpair, blocks, qblock, window = pair_ref.shape
     margin = window // 2 - qblock // 2 + qblock
@@ -96,7 +99,9 @@
     mid_ref[...] = mid.astype(BF).reshape(samples, atoms, channels)
 
 
-def atom_attention(feats, before, after, pair, shift, offset, limit, gain, qkv, out_proj, wpair):
+def atom_attention(
+    feats, before, after, pair, shift, offset, limit, gain, qkv, out_proj, wpair, others=()
+):
     samples, atoms, channels = feats.shape
     blocks, qblock, window = pair.shape[1:]
     rows = atoms + 2 * (window // 2 - qblock // 2 + qblock)
@@ -108,9 +113,10 @@
         functools.partial(atom_kernel, limit_atoms=limit),
         grid=(samples // step,),
         in_specs=[smem, smem, smem, part(feats), part(before), part(after), whole(pair),
-                  whole(gain), whole(qkv), whole(out_proj)],
-        out_specs=part(feats),
-        out_shape=jax.ShapeDtypeStruct(feats.shape, BF),
+                  whole(gain), whole(qkv), whole(out_proj)]
+        + [pl.BlockSpec(memory_space=pl.ANY)] * len(others),
+        out_specs=[part(feats), pl.BlockSpec((8, 128), lambda i: (0, 0))],
+        out_shape=[jax.ShapeDtypeStruct(feats.shape, BF), jax.ShapeDtypeStruct((8, 128), F32)],
         scratch_shapes=[
             pltpu.VMEM((blocks, qblock * wpair.shape[1], window), F32),
             pltpu.VMEM((step, rows, 2 * channels), BF),
@@ -118,72 +124,62 @@
         compiler_params=params(),
         cost_estimate=pl.CostEstimate(flops=8_000_000_000, bytes_accessed=3_000_000, transcendentals=1_000_000),
         name="atom_attention",
-    )(shift, offset, wpair, feats, before, after, pair, gain, qkv, out_proj)
-
-
-def tie(value, *others):
-    def kernel(*refs):
+    )(shift, offset, wpair, feats, before, after, pair, gain, qkv, out_proj, *others)
+
+
+def tie(value, after):
+    def kernel(value_ref, after_ref, out_ref):
         pass
+
     hbm = pl.BlockSpec(memory_space=pl.ANY)
     return pl.pallas_call(
         kernel,
-        in_specs=[hbm] * (1 + len(others)),
+        in_specs=[hbm] * 2,
         out_specs=hbm,
         out_shape=jax.ShapeDtypeStruct(value.shape, value.dtype),
         input_output_aliases={0: 0},
         name="tie",
-    )(value, *others)
-
-
-def tie(value, *others):
-    def kernel(*refs):
-        pass
-    hbm = pl.BlockSpec(memory_space=pl.ANY)
-    return pl.pallas_call(
-        kernel,
-        in_specs=[hbm] * (1 + len(others)),
-        out_specs=hbm,
-        out_shape=jax.ShapeDtypeStruct(value.shape, value.dtype),
-        input_output_aliases={0: 0},
-        name="tie",
-    )(value, *others)
-
-
-def split_kernel(value_ref, after_ref, first_ref, rest_ref, sems):
+    )(value, after)
+
+
+def split_kernel(value_ref, after_ref, first_ref, rest_ref):
     rows = first_ref.shape[0]
-    copies = [
-        pltpu.make_async_copy(value_ref.at[pl.ds(0, rows)], first_ref, sems.at[0]),
-        pltpu.make_async_copy(value_ref.at[pl.ds(rows, rest_ref.shape[0])], rest_ref, sems.at[1]),
-    ]
-    for copy in copies:
-        copy.start()
-    for copy in copies:
-        copy.wait()
+    first_ref[...] = value_ref[:rows]
+    rest_ref[...] = value_ref[rows:]
 
 
 def split_rows(value, rows, after):
-    hbm = pl.BlockSpec(memory_space=pl.ANY)
+    vmem = pl.BlockSpec(memory_space=pltpu.VMEM)
     total, width = value.shape
     return pl.pallas_call(
         split_kernel,
-        in_specs=[pl.BlockSpec(memory_space=pltpu.VMEM), hbm],
-        out_specs=[hbm] * 2,
+        in_specs=[vmem, pl.BlockSpec(memory_space=pl.ANY)],
+        out_specs=[vmem] * 2,
         out_shape=[
             jax.ShapeDtypeStruct((rows, width), value.dtype),
             jax.ShapeDtypeStruct((total - rows, width), value.dtype),
         ],
-        scratch_shapes=[pltpu.SemaphoreType.DMA((2,))],
         cost_estimate=pl.CostEstimate(flops=0, bytes_accessed=4 * value.size, transcendentals=0),
         name="split_rows",
     )(value, after)
 
 
+def source_of(place_ref, i, peers):
+    chips = peers // 2
+    core = place_ref[1] if i < chips else 1 - place_ref[1]
+    return lax.rem(place_ref[0] + chips - i % chips, chips) * 2 + core
+
+
 def token_kernel(
-    mid_ref, count_row_ref, count_col_ref, pool_ref, gain_ref, w_hbm, qkv_ref, gate_ref,
-    single_ref, normed_ref, w_ref, sem, *, head_dim,
+    place_ref, mid_ref, count_row_ref, count_col_ref, pool_ref, gain_ref, *refs, head_dim, parts,
 ):
-    load = pltpu.make_async_copy(w_hbm, w_ref, sem)
-    load.start()
+    qkv_ref, gate_ref, single_ref, normed_ref, w_ref, sems = refs[-6:]
+    loads = []
+    for i, (slot, row, rows) in enumerate(parts):
+        dst = w_ref.at[slot, pl.ds(row, rows)]
+        loads.append(pltpu.make_async_copy(refs[i], dst, sems.at[i]))
+    for load in loads:
+        load.start()
     peers, samples, atoms, channels = mid_ref.shape
     toks = count_col_ref.shape[0]
     total = peers * atoms
@@ -203,12 +199,14 @@
         single_ref[s] = single
         normed_ref[s * toks : (s + 1) * toks, :] = layer_norm(single, gain_ref[...]).astype(BF)
 
-    load.wait()
+    for load in loads:
+        load.wait()
     scale = LOG2E / float(np.sqrt(head_dim))
     width = w_ref.shape[1] // 4
     local = width // head_dim
-    for p in range(peers):
-        turned = dot(w_ref[p], normed_ref[...], (1, 1))
+    for i in range(peers):
+        p = source_of(place_ref, i, peers)
+        turned = dot(w_ref[i], normed_ref[...], (1, 1))
         for hh in range(local):
             for s in range(samples):
                 for f in range(4):
@@ -222,7 +220,7 @@
                         gate_ref[p * local + hh, s] = tile.astype(BF)
 
 
-def pool_and_project(mid, count, pool, gain, w, heads):
+def pool_and_project(place, mid, count, pool, gain, pieces, heads, others):
     peers, samples, atoms, channels = mid.shape
     toks = count.shape[0]
     width = pool.shape[1]
@@ -231,9 +229,11 @@
     row, col = count.reshape(1, toks), count.reshape(toks, 1)
     gain = gain.reshape(1, width)
     vmem = pl.BlockSpec(memory_space=pltpu.VMEM)
-    return pl.pallas_call(
-        functools.partial(token_kernel, head_dim=head_dim),
-        in_specs=[vmem] * 5 + [pl.BlockSpec(memory_space=pl.ANY)],
+    hbm = pl.BlockSpec(memory_space=pl.ANY)
+    parts = tuple((slot, first, array.shape[0]) for slot, first, array in pieces)
+    return pl.pallas_call(
+        functools.partial(token_kernel, head_dim=head_dim, parts=parts),
+        in_specs=[pl.BlockSpec(memory_space=pltpu.SMEM)] + [vmem] * 5 + [hbm] * (len(pieces) + len(others)),
         out_specs=[vmem] * 3,
         out_shape=[
             jax.ShapeDtypeStruct((heads, samples, 3, head_dim, toks), BF),
@@ -242,25 +242,25 @@
         ],
         scratch_shapes=[
             pltpu.VMEM((samples * toks, width), BF),
-            pltpu.VMEM(w.shape, BF),
-            pltpu.SemaphoreType.DMA,
+            pltpu.VMEM((peers,) + pieces[0][2].shape, BF),
+            pltpu.SemaphoreType.DMA((len(pieces),)),
         ],
-        compiler_params=pltpu.CompilerParams(vmem_limit_bytes=VMEM_LIMIT),
+        compiler_params=pltpu.CompilerParams(vmem_limit_bytes=VMEM_MOST),
         cost_estimate=pl.CostEstimate(flops=6_000_000_000, bytes_accessed=8_000_000, transcendentals=1000),
         name="pool_and_project",
-    )(mid, row, col, pool, gain, w)
-
-
-def attend_kernel(place_ref, qkv_ref, gathered_ref, *refs, gathered_rows):
-    pieces, (out_ref, keys_ref, values_ref) = refs[:-3], refs[-3:]
+    )(place, mid, row, col, pool, gain, *[array for _, _, array in pieces], *others)
+
+
+def attend_kernel(place_ref, qkv_ref, *refs):
+    out_ref, keys_ref, values_ref = refs[-3:]
+    half = (len(refs) - 3) // 2
+    upper, lower = refs[:half], refs[half : 2 * half]
     peers, samples, _, head_dim, toks = qkv_ref.shape
     qblocks = out_ref.shape[0]
-    width = gathered_ref.shape[2]
+    width = upper[0].shape[1]
     per = width // toks
     step = pl.program_id(0)
-    first = gathered_rows // (qblocks * toks)
-    chip, core = place_ref[0], place_ref[1]
-    chips = len(pieces) // 2
+    first = pl.num_programs(0) // 2
 
     def load(order):
         for s in range(samples):
@@ -292,54 +292,48 @@
 
     @pl.when(step == 0)
     def _():
-        load(list(range(peers)))
-
-    @pl.when(step == first)
-    def _():
-        order = []
-        for i in range(2 * chips):
-            source = lax.rem(chip + chips - i % chips, chips) * 2 + (core if i < chips else 1 - core)
-            order += [source * per + j for j in range(per)]
-        load(order)
+        sources = [source_of(place_ref, i, half) for i in range(half)]
+        load([source * per + j for source in sources for j in range(per)])
 
     @pl.when(step < first)
     def _():
-        attend([gathered_ref.at[c] for c in range(gathered_ref.shape[0])])
+        attend(upper)
 
     @pl.when(step >= first)
     def _():
-        attend(pieces)
-
-
-def token_attention(place, qkv, gathered, pieces):
+        attend(lower)
+
+
+def token_attention(place, qkv, upper, lower):
     peers, samples, _, head_dim, toks = qkv.shape
-    cols, rows, width = gathered.shape
+    rows, width = upper[0].shape
     qblocks = 4
     tile = qblocks * toks
     keys = peers * toks
     first = rows // tile
+    early = lambda i: (jnp.minimum(i, first - 1), 0)
     late = lambda i: (jnp.maximum(i - first, 0), 0)
     return pl.pallas_call(
-        functools.partial(attend_kernel, gathered_rows=rows),
+        attend_kernel,
         grid=(keys // tile,),
         in_specs=[
             pl.BlockSpec(memory_space=pltpu.SMEM),
             pl.BlockSpec(qkv.shape, lambda i: (0, 0, 0, 0, 0)),
-            pl.BlockSpec((cols, tile, width), lambda i: (0, jnp.minimum(i, first - 1), 0)),
-        ] + [pl.BlockSpec((tile, width), late)] * len(pieces),
+        ] + [pl.BlockSpec((tile, width), early)] * len(upper)
+        + [pl.BlockSpec((tile, width), late)] * len(lower),
         out_specs=pl.BlockSpec((qblocks, samples, head_dim, toks), lambda i: (i, 0, 0, 0)),
         out_shape=jax.ShapeDtypeStruct((peers, samples, head_dim, toks), BF),
         scratch_shapes=[
             pltpu.VMEM((samples, head_dim, keys), BF),
             pltpu.VMEM((samples, head_dim + 16, keys), BF),
         ],
-        compiler_params=params(58 * 1024 * 1024),
+        compiler_params=params(VMEM_MOST),
         cost_estimate=pl.CostEstimate(
             flops=4 * samples * keys * keys * 128, bytes_accessed=2 * keys * keys + 2 * qkv.size,
             transcendentals=samples * keys * keys,
         ),
         name="token_attention",
-    )(place, qkv, gathered, *pieces)
+    )(place, qkv, *upper, *lower)
 
 
 def out_kernel(mixed_ref, gate_ref, single_ref, out_proj_ref, return_ref, back_ref):
@@ -401,8 +395,19 @@
     before = lax.ppermute(atom_feats, ("seq", "col"), up)
     after = lax.ppermute(atom_feats, ("seq", "col"), down)
 
-    turned_w = jnp.transpose(token_qkvg, (1, 2, 0)).reshape(-1, width)
-    all_w = lax.all_gather(turned_w, "col", axis=0)
+    chips = peers // 2
+    col = lax.axis_index("col")
+    place = jnp.stack([col // 2, col % 2]).astype(jnp.int32)
+
+    def along(value, hop):
+        pairs = [(2 * x + k, 2 * ((x + hop) % chips) + k) for x in range(chips) for k in range(2)]
+        return lax.ppermute(value, "col", pairs)
+
+    def across(value):
+        return lax.ppermute(value, "col", [(i, i ^ 1) for i in range(peers)])
+
+    own_w = jnp.transpose(token_qkvg, (1, 2, 0)).reshape(-1, width)
+    back_w, ahead_w = along(own_w, 1), along(own_w, -1)
 
     tile_bias = jnp.einsum("ijc,ch->hij", pair_tiles, pair_proj, preferred_element_type=F32)
     tile_bias = (tile_bias * LOG2E).astype(BF)
@@ -410,28 +415,29 @@
 
     index = lax.axis_index(("seq", "col"))
     offset = (index * atoms).astype(jnp.int32).reshape(1)
-    mid = atom_attention(
+    mid, done = atom_attention(
         atom_feats, before, after, atom_pair, key_shift, offset, atoms * devices,
         atom_gain.reshape(1, -1), atom_qkv, atom_out_proj, atom_pair_proj.astype(F32),
-    )
-    chips = peers // 2
-    first, rest = split_rows(head_bias.reshape(seqs * toks, -1), 3 * seqs * toks // 4, mid)
-    gathered = lax.all_gather(first, "col", axis=0)
-
+        (back_w, ahead_w),
+    )
     mine = lax.all_to_all(
         mid.reshape(peers, samples // peers, atoms, channels), "col", split_axis=0, concat_axis=0, tiled=True
     )
-    qkv, gate, single = pool_and_project(mine, token_count, pool_proj, token_gain, all_w, heads)
-    pieces = [tie(rest, single)]
-    for hop in range(1, chips):
-        pairs = [(2 * x + k, 2 * ((x + hop) % chips) + k) for x in range(chips) for k in range(2)]
-        pieces.append(lax.ppermute(pieces[0], "col", pairs))
-    swap = [(i, i ^ 1) for i in range(peers)]
-    pieces += [lax.ppermute(piece, "col", swap) for piece in pieces]
+    half = seqs * toks // 2
+    upper, lower = split_rows(head_bias.reshape(seqs * toks, -1), half, done)
+    pieces = [(0, 0, own_w), (1, 0, back_w), (2, 0, tie(along(own_w, 2), upper)), (3, 0, ahead_w)]
+    pieces += [(slot + chips, first, across(array)) for slot, first, array in pieces]
+    back_upper, ahead_lower = along(upper, 1), along(lower, -1)
+    qkv, gate, single = pool_and_project(
+        place, mine, token_count, pool_proj, token_gain, pieces, heads, (back_upper, ahead_lower)
+    )
+    back_lower, ahead_upper = along(lower, 1), along(upper, -1)
+    uppers = [upper, back_upper, along(back_upper, 1), ahead_upper]
+    lowers = [lower, back_lower, along(ahead_lower, -1), ahead_lower]
     qkv = lax.all_to_all(qkv, "seq", split_axis=0, concat_axis=0, tiled=True)
-    col = lax.axis_index("col")
-    place = jnp.stack([col // 2, col % 2]).astype(jnp.int32)
-    mixed = token_attention(place, qkv, gathered, pieces)
+    uppers += [across(piece) for piece in uppers]
+    lowers += [across(piece) for piece in lowers]
+    mixed = token_attention(place, qkv, uppers, lowers)
     mixed = lax.all_to_all(mixed, "seq", split_axis=0, concat_axis=0, tiled=True)
     back = out_project(mixed, gate, single, token_out_proj, return_proj)
     back = lax.all_gather(back, "col", axis=0, tiled=True)

time: 157 us -> 150 us (0.955)
  between operations: 13.8 us -> 0.31 us
  starting transfers between devices: 43.4 us -> 55.9 us
  waiting for transfers between devices: 41 us -> 30.4 us
  local copies, waits for them, and re-layouts: 3.51 us -> 6.52 us
  Pallas kernels: 33.6 us -> 35.3 us
    ppermute x7 -> x21, starting transfers between devices: 11.4 us -> 27.6 us  [the longest x9 15.7 us: along(): return lax.ppermute(value, 'col', pairs)]
    all_to_all x1, waiting for transfers between devices: 6.04 us -> 0.01 us  [shards(): lax.all_to_all(tile_bias, 'seq', split_axis=0, concat_axis=0, tiled=True)]
    all_to_all x1, starting transfers between devices: 8.22 us -> 3.84 us  [shards(): lax.all_to_all(mid.reshape(peers, samples // peers, atoms, channels), 'co...]
    ppermute x7 -> x21, waiting for transfers between devices: 13.4 us -> 11.1 us  [the longest x9 9.67 us: along(): return lax.ppermute(value, 'col', pairs)]
    all_gather x2 -> x0, waiting for transfers between devices: 2.08 us -> none  [the longest x1 2.08 us: shards(): gathered = lax.all_gather(first, 'col', axis=0)]
    unnamed x50 -> x60, local copies, waits for them, and re-layouts: 1.84 us -> 3.67 us
  transfers between devices with their start and end apart: 15 -> 27, of which waited for: 7 -> 5; matrix products, arithmetic and copies ran while one was open for 5% -> 6% of each run, Pallas kernels for 10% -> 11%
where the time goes in v1:
time: 150 us
  starting transfers between devices  55.9 us (37%)
  Pallas kernels  35.3 us (24%)
  waiting for transfers between devices  30.4 us (20%)
  blocking collectives  14.5 us (10%)
  local copies, waits for them, and re-layouts  6.52 us (4%)
  matrix products  5.66 us (4%)
    ppermute x9, starting transfers between devices, along(): return lax.ppermute(value, 'col', pairs)  15.7 us
    pallas_call x1, Pallas kernels, token_attention(): pl.pallas_call(attend_kernel, grid=(keys // tile,), in_specs=[pl.BlockSpe...  15.6 us
    all_gather x1, blocking collectives, shards(): back = lax.all_gather(back, 'col', axis=0, tiled=True)  14.5 us
    ppermute x12, starting transfers between devices, across(): return lax.ppermute(value, 'col', [(i, i ^ 1) for i in range(peers)])  11.9 us
    all_to_all x1, waiting for transfers between devices, shards(): lax.all_to_all(mid.reshape(peers, samples // peers, atoms, channels), 'co...  10.1 us
    ppermute x9, waiting for transfers between devices, along(): return lax.ppermute(value, 'col', pairs)  9.67 us
    all_to_all x1, waiting for transfers between devices, shards(): lax.all_to_all(mixed, 'seq', split_axis=0, concat_axis=0, tiled=True)  9.1 us
    pallas_call x1, Pallas kernels, atom_attention(): pl.pallas_call(functools.partial(atom_kernel, limit_atoms=limit), grid=(s...  8.01 us
  transfers between devices with their start and end apart: 27, of which 5 were waited for; matrix products, arithmetic and copies ran while one was open for 6% of the time, Pallas kernels for 11%

profile of v1, /device:TPU:1, one launch (start us, length us, event | category | flops | bytes accessed | tf_op | source)
XLA Modules:
  0.0 149.6 jit_solution(11144441313071202774)
XLA Ops:
  0.0 2.0 %collective-permute-start.2 = (bf16[384,768]{1,0:T(8,128)(2,1)}, bf16[384,768]{1,0:T(8,128)(2,1)S(1)}, u32[]{:S(2)}, u32[]{:S(2)}) collective-permute-start(bf16[384,768]{1,0:T(8,128)(2,1)} %bitcast.20), channel_id=1, source_target_pairs={{0,2},{1,3},{2,4},{3,5},{4,6},{5,7},{6,0},{7,1},{8,10},{9,11},{10,... | collective-permute-start | bytes 1769480 | tf_op jit(solution)/shard_map/ppermute | solution.py:404
  2.0 1.3 collective-permute-start.3
  3.4 3.1 %collective-permute-start = (bf16[16,128,128]{2,1,0:T(8,128)(2,1)}, bf16[16,128,128]{2,1,0:T(8,128)(2,1)S(1)}, u32[]{:S(2)}, u32[]{:S(2)}) collective-permute-start(bf16[16,128,128]{2,1,0:T(8,128)(2,1)} %feats_ref.1), channel_id=1, source_target_pairs={{0,1},{1,2},{2,3},{3,4},{4,5},{5,6},{6,7},{7,8},{8,9},{9,10},{10,1... | collective-permute-start | bytes 1572872 | tf_op jit(solution)/shard_map/ppermute | solution.py:395
  6.5 1.9 %collective-permute-start.1 = (bf16[16,128,128]{2,1,0:T(8,128)(2,1)}, bf16[16,128,128]{2,1,0:T(8,128)(2,1)S(1)}, u32[]{:S(2)}, u32[]{:S(2)}) collective-permute-start(bf16[16,128,128]{2,1,0:T(8,128)(2,1)} %feats_ref.1), channel_id=1, source_target_pairs={{1,0},{2,1},{3,2},{4,3},{5,4},{6,5},{7,6},{8,7},{9,8},{10,9},{11,1... | collective-permute-start | bytes 1572872 | tf_op jit(solution)/shard_map/ppermute | solution.py:396
  8.5 5.7 %multiply_convert_fusion = bf16[16,128,256]{2,0,1:T(8,128)(2,1)S(1)} fusion(bf16[128,256,128]{2,1,0:T(8,128)(2,1)} %param.28, bf16[128,16]{0,1:T(8,128)(2,1)S(1)} %copy-done), kind=kOutput, calls=%fused_computation | convolution fusion | flops 135266304 | bytes 9441280 | tf_op jit(solution)/shard_map/ijc,ch->hij/dot_general | solution.py:412
  14.2 1.3 copy.27
  15.6 7.9 %all-to-all-start.1 = ((bf16[16,128,256]{2,1,0:T(8,128)(2,1)}), bf16[16,128,256]{2,1,0:T(8,128)(2,1)}, u32[]{:S(2)}, u32[]{:S(2)}) async-start(bf16[16,128,256]{2,1,0:T(8,128)(2,1)} %copy.27), calls=%async_computation.1 | async-start | bytes 2097152 | tf_op jit(solution)/shard_map/all_to_all | solution.py:414
  23.5 2.4 %collective-permute-start.4 = (bf16[384,768]{1,0:T(8,128)(2,1)}, bf16[384,768]{1,0:T(8,128)(2,1)}, u32[]{:S(2)}, u32[]{:S(2)}) collective-permute-start(bf16[384,768]{1,0:T(8,128)(2,1)} %bitcast.22), channel_id=1, source_target_pairs={{0,4},{1,5},{2,6},{3,7},{4,0},{5,1},{6,2},{7,3},{8,12},{9,13},{10,... | collective-permute-start | bytes 1769480 | tf_op jit(solution)/shard_map/ppermute | solution.py:404
  26.0 1.8 %collective-permute-start.5 = (bf16[384,768]{1,0:T(8,128)(2,1)}, bf16[384,768]{1,0:T(8,128)(2,1)}, u32[]{:S(2)}, u32[]{:S(2)}) collective-permute-start(bf16[384,768]{1,0:T(8,128)(2,1)} %bitcast.23), channel_id=1, source_target_pairs={{0,1},{1,0},{2,3},{3,2},{4,5},{5,4},{6,7},{7,6},{8,9},{9,8},{10,11... | collective-permute-start | bytes 1769480 | tf_op jit(solution)/shard_map/ppermute | solution.py:407
  28.4 8.0 %atom_attention.1 = (bf16[16,128,128]{2,1,0:T(8,128)(2,1)}, f32[8,128]{1,0:T(8,128)S(1)}) custom-call(s32[4]{0:T(128)S(1)} %copy-done.12, s32[1]{0:T(128)} %bitcast.3.off_ref, f32[16,4]{1,0:T(8,128)S(1)} %copy.26.wpair_ref, bf16[16,128,128]{2,1,0:T(8,128)(2,1)S(1)} %copy-done.8, bf16[16,128,128]{2,1,0:T(8,128)(2,1)S(1)} %collective-permute-done.before_ref, ...), custom_call_target="tpu_custom_call" | custom-call | flops 8000000000 | bytes 3000000 | tf_op jit(solution)/shard_map/atom_attention/pallas_call | solution.py:112
  37.0 2.3 %split_rows.1 = (bf16[1024,256]{1,0:T(8,128)(2,1)}, bf16[1024,256]{1,0:T(8,128)(2,1)}) custom-call(bf16[2048,256]{1,0:T(8,128)(2,1)} %bitcast.12.value_ref, f32[8,128]{1,0:T(8,128)} %copy-done.5), custom_call_target="tpu_custom_call" | custom-call | bytes 2097152 | tf_op jit(solution)/shard_map/split_rows/pallas_call | solution.py:154
  39.3 4.6 %collective-permute-start.7 = (bf16[384,768]{1,0:T(8,128)(2,1)}, bf16[384,768]{1,0:T(8,128)(2,1)S(1)}, u32[]{:S(2)}, u32[]{:S(2)}) collective-permute-start(bf16[384,768]{1,0:T(8,128)(2,1)} %tie.1.refs_2_), channel_id=1, source_target_pairs={{0,1},{1,0},{2,3},{3,2},{4,5},{5,4},{6,7},{7,6},{8,9},{9,8},{10,11... | collective-permute-start | bytes 1769480 | tf_op jit(solution)/shard_map/ppermute | solution.py:407
  43.9 1.7 %collective-permute-start.9 = (bf16[1024,256]{1,0:T(8,128)(2,1)}, bf16[1024,256]{1,0:T(8,128)(2,1)S(1)}, u32[]{:S(2)}, u32[]{:S(2)}) collective-permute-start(bf16[1024,256]{1,0:T(8,128)(2,1)} %get-tuple-element.14.after_ref.refs_0_), channel_id=1, source_target_pairs={{0,2},{1,3},{2,4},{3,5},{4,6},{5,7},{6,0},{7,1},{8,10},{9,11},{10,... | collective-permute-start | bytes 1572872 | tf_op jit(solution)/shard_map/ppermute | solution.py:404
  45.6 2.9 %collective-permute-start.10 = (bf16[1024,256]{1,0:T(8,128)(2,1)}, bf16[1024,256]{1,0:T(8,128)(2,1)}, u32[]{:S(2)}, u32[]{:S(2)}) collective-permute-start(bf16[1024,256]{1,0:T(8,128)(2,1)} %get-tuple-element.15.refs_8_), channel_id=1, source_target_pairs={{0,6},{1,7},{2,0},{3,1},{4,2},{5,3},{6,4},{7,5},{8,14},{9,15},{10,... | collective-permute-start | bytes 1572872 | tf_op jit(solution)/shard_map/ppermute | solution.py:404
  48.5 3.8 %all-to-all-start = ((bf16[8,2,128,128]{3,2,1,0:T(8,128)(2,1)}), bf16[8,2,128,128]{3,2,1,0:T(8,128)(2,1)S(1)}, u32[]{:S(2)}, u32[]{:S(2)}) async-start(bf16[8,2,128,128]{3,2,1,0:T(8,128)(2,1)} %bitcast.8), calls=%async_computation | async-start | bytes 1048576 | tf_op jit(solution)/shard_map/all_to_all | solution.py:423
  54.8 2.6 %collective-permute-start.12 = (bf16[1024,256]{1,0:T(8,128)(2,1)S(1)}, bf16[1024,256]{1,0:T(8,128)(2,1)}, u32[]{:S(2)}, u32[]{:S(2)}) collective-permute-start(bf16[1024,256]{1,0:T(8,128)(2,1)S(1)} %copy-done.14), channel_id=1, source_target_pairs={{0,6},{1,7},{2,0},{3,1},{4,2},{5,3},{6,4},{7,5},{8,14},{9,15},{10,... | collective-permute-start | bytes 1572872 | tf_op jit(solution)/shard_map/ppermute | solution.py:404
  57.4 10.1 %all-to-all-done.mid_ref = bf16[8,2,128,128]{3,2,1,0:T(8,128)(2,1)S(1)} async-done(((bf16[8,2,128,128]{3,2,1,0:T(8,128)(2,1)}), bf16[8,2,128,128]{3,2,1,0:T(8,128)(2,1)S(1)}, u32[]{:S(2)}, u32[]{:S(2)}) %all-to-all-start) | async-done | bytes 524320 | tf_op jit(solution)/shard_map/all_to_all | solution.py:423
  68.7 6.4 %pool_and_project.1 = (bf16[16,2,3,48,128]{4,3,2,1,0:T(8,128)(2,1)}, bf16[16,2,48,128]{3,2,1,0:T(8,128)(2,1)}, f32[2,128,768]{2,1,0:T(8,128)}) custom-call(s32[2]{0:T(128)} %pad_add_fusion.place_ref, bf16[8,2,128,128]{3,2,1,0:T(8,128)(2,1)} %copy-done.15, f32[1,128]{1,0:T(1,128)} %get-tuple-element.20.count_row_ref, f32[128,1]{1,0:T(8,128)} %copy.28.count_col_ref, ...), custom_call_target="tpu_custom_call" | custom-call | flops 6000000000 | bytes 8000000 | tf_op jit(solution)/shard_map/pool_and_project/pallas_call | solution.py:234
  75.1 4.6 %all-to-all-start.2 = ((bf16[16,2,3,48,128]{4,3,2,1,0:T(8,128)(2,1)}), bf16[16,2,3,48,128]{4,3,2,1,0:T(8,128)(2,1)}, u32[]{:S(2)}, u32[]{:S(2)}) async-start(bf16[16,2,3,48,128]{4,3,2,1,0:T(8,128)(2,1)} %get-tuple-element.16), calls=%async_computation.2 | async-start | bytes 2359296 | tf_op jit(solution)/shard_map/all_to_all | solution.py:437
  79.8 1.4 collective-permute-start.13
  81.3 1.2 collective-permute-start.11
  82.4 1.5 collective-permute-start.18
  83.9 1.0 collective-permute-start.14
  86.2 9.7 %collective-permute-done.11.refs_2_ = bf16[1024,256]{1,0:T(8,128)(2,1)S(1)} collective-permute-done((bf16[1024,256]{1,0:T(8,128)(2,1)}, bf16[1024,256]{1,0:T(8,128)(2,1)S(1)}, u32[]{:S(2)}, u32[]{:S(2)}) %collective-permute-start.11) | collective-permute-done | bytes 524320 | tf_op jit(solution)/shard_map/ppermute | solution.py:404
  95.9 1.1 collective-permute-start.20
  97.9 0.8 collective-permute-done.20.refs_13_
  99.6 0.8 copy-done.27
  100.4 15.6 %token_attention.1 = bf16[16,2,48,128]{3,2,1,0:T(8,128)(2,1)} custom-call(s32[2]{0:T(128)} %pad_add_fusion.place_ref, bf16[16,2,3,48,128]{4,3,2,1,0:T(8,128)(2,1)} %all-to-all-done.2.qkv_ref, bf16[1024,256]{1,0:T(8,128)(2,1)} %get-tuple-element.14.after_ref.refs_0_, bf16[1024,256]{1,0:T(8,128)(2,1)} %copy-done.19, bf16[1024,256]{1,0:T(8,128)(2,1)} %copy-done.21, ...), custom_call_target="tpu_custom_call" | custom-call | flops 4294967296 | bytes 9568256 | tf_op jit(solution)/shard_map/token_attention/pallas_call | solution.py:316
  116.0 6.8 %all-to-all-start.3 = ((bf16[16,2,48,128]{3,2,1,0:T(8,128)(2,1)}), bf16[16,2,48,128]{3,2,1,0:T(8,128)(2,1)S(1)}, u32[]{:S(2)}, u32[]{:S(2)}) async-start(bf16[16,2,48,128]{3,2,1,0:T(8,128)(2,1)} %token_attention.1), calls=%async_computation.3 | async-start | bytes 786432 | tf_op jit(solution)/shard_map/all_to_all | solution.py:441
  123.0 9.1 %all-to-all-done.3.mixed_ref = bf16[16,2,48,128]{3,2,1,0:T(8,128)(2,1)S(1)} async-done(((bf16[16,2,48,128]{3,2,1,0:T(8,128)(2,1)}), bf16[16,2,48,128]{3,2,1,0:T(8,128)(2,1)S(1)}, u32[]{:S(2)}, u32[]{:S(2)}) %all-to-all-start.3) | async-done | bytes 393248 | tf_op jit(solution)/shard_map/all_to_all | solution.py:441
  133.0 14.5 %all_gather.3.back_ref = bf16[16,128,128]{2,1,0:T(8,128)(2,1)S(1)} all-gather(bf16[2,128,128]{2,1,0:T(8,128)(2,1)S(1)} %out_project.1), channel_id=1, replica_groups=mesh['seq'=16,'col'=8] {'col'}, dimensions={0}, use_global_device_ids=true | all-gather | bytes 589824 | tf_op jit(solution)/shard_map/all_gather | solution.py:443
  147.4 2.2 %spread_back.1 = bf16[16,128,128]{2,1,0:T(8,128)(2,1)} custom-call(s32[128,1]{1,0:T(8,128)S(1)} %copy.29.tok_ref, bf16[16,128,128]{2,1,0:T(8,128)(2,1)S(1)} %all_gather.3.back_ref, bf16[16,128,128]{2,1,0:T(8,128)(2,1)} %get-tuple-element.12.mid_ref), custom_call_target="tpu_custom_call" | custom-call | flops 100000000 | bytes 2000000 | tf_op jit(solution)/shard_map/spread_back/pallas_call | solution.py:369
  (99 shorter events, 8.9 us)
Async XLA Ops:
  0.0 27.8 %collective-permute-start.2 = (bf16[384,768]{1,0:T(8,128)(2,1)}, bf16[384,768]{1,0:T(8,128)(2,1)S(1)}, u32[]{:S(2)}, u32[]{:S(2)}) collective-permute-start(bf16[384,768]{1,0:T(8,128)(2,1)} %bitcast.20), channel_id=1, source_target_pairs={{0,2},{1,3},{2,4},{3,5},{4,6},{5,7},{6,0},{7,1},{8,10},{9,11},{10,... | collective-permute-start | bytes 1769480 | tf_op jit(solution)/shard_map/ppermute | solution.py:404
  2.0 25.9 %collective-permute-start.3 = (bf16[384,768]{1,0:T(8,128)(2,1)}, bf16[384,768]{1,0:T(8,128)(2,1)S(1)}, u32[]{:S(2)}, u32[]{:S(2)}) collective-permute-start(bf16[384,768]{1,0:T(8,128)(2,1)} %bitcast.21), channel_id=1, source_target_pairs={{0,6},{1,7},{2,0},{3,1},{4,2},{5,3},{6,4},{7,5},{8,14},{9,15},{10,... | collective-permute-start | bytes 1769480 | tf_op jit(solution)/shard_map/ppermute | solution.py:404
  3.4 22.6 %collective-permute-start = (bf16[16,128,128]{2,1,0:T(8,128)(2,1)}, bf16[16,128,128]{2,1,0:T(8,128)(2,1)S(1)}, u32[]{:S(2)}, u32[]{:S(2)}) collective-permute-start(bf16[16,128,128]{2,1,0:T(8,128)(2,1)} %feats_ref.1), channel_id=1, source_target_pairs={{0,1},{1,2},{2,3},{3,4},{4,5},{5,6},{6,7},{7,8},{8,9},{9,10},{10,1... | collective-permute-start | bytes 1572872 | tf_op jit(solution)/shard_map/ppermute | solution.py:395
  6.5 21.8 %collective-permute-start.1 = (bf16[16,128,128]{2,1,0:T(8,128)(2,1)}, bf16[16,128,128]{2,1,0:T(8,128)(2,1)S(1)}, u32[]{:S(2)}, u32[]{:S(2)}) collective-permute-start(bf16[16,128,128]{2,1,0:T(8,128)(2,1)} %feats_ref.1), channel_id=1, source_target_pairs={{1,0},{2,1},{3,2},{4,3},{5,4},{6,5},{7,6},{8,7},{9,8},{10,9},{11,1... | collective-permute-start | bytes 1572872 | tf_op jit(solution)/shard_map/ppermute | solution.py:396
  15.6 21.5 %all-to-all-start.1 = ((bf16[16,128,256]{2,1,0:T(8,128)(2,1)}), bf16[16,128,256]{2,1,0:T(8,128)(2,1)}, u32[]{:S(2)}, u32[]{:S(2)}) async-start(bf16[16,128,256]{2,1,0:T(8,128)(2,1)} %copy.27), calls=%async_computation.1 | async-start | bytes 2097152 | tf_op jit(solution)/shard_map/all_to_all | solution.py:414
  23.5 15.8 %collective-permute-start.4 = (bf16[384,768]{1,0:T(8,128)(2,1)}, bf16[384,768]{1,0:T(8,128)(2,1)}, u32[]{:S(2)}, u32[]{:S(2)}) collective-permute-start(bf16[384,768]{1,0:T(8,128)(2,1)} %bitcast.22), channel_id=1, source_target_pairs={{0,4},{1,5},{2,6},{3,7},{4,0},{5,1},{6,2},{7,3},{8,12},{9,13},{10,... | collective-permute-start | bytes 1769480 | tf_op jit(solution)/shard_map/ppermute | solution.py:404
  26.0 19.6 %collective-permute-start.5 = (bf16[384,768]{1,0:T(8,128)(2,1)}, bf16[384,768]{1,0:T(8,128)(2,1)}, u32[]{:S(2)}, u32[]{:S(2)}) collective-permute-start(bf16[384,768]{1,0:T(8,128)(2,1)} %bitcast.23), channel_id=1, source_target_pairs={{0,1},{1,0},{2,3},{3,2},{4,5},{5,4},{6,7},{7,6},{8,9},{9,8},{10,11... | collective-permute-start | bytes 1769480 | tf_op jit(solution)/shard_map/ppermute | solution.py:407
  27.9 26.9 %collective-permute-start.6 = (bf16[384,768]{1,0:T(8,128)(2,1)S(1)}, bf16[384,768]{1,0:T(8,128)(2,1)}, u32[]{:S(2)}, u32[]{:S(2)}) collective-permute-start(bf16[384,768]{1,0:T(8,128)(2,1)S(1)} %collective-permute-done.2.refs_0_.refs_1_), channel_id=1, source_target_pairs={{0,1},{1,0},{2,3},{3,2},{4,5},{5,4},{6,7},{7,6},{8,9},{9,8},{10,11... | collective-permute-start | bytes 1769480 | tf_op jit(solution)/shard_map/ppermute | solution.py:407
  28.0 29.4 %collective-permute-start.8 = (bf16[384,768]{1,0:T(8,128)(2,1)S(1)}, bf16[384,768]{1,0:T(8,128)(2,1)}, u32[]{:S(2)}, u32[]{:S(2)}) collective-permute-start(bf16[384,768]{1,0:T(8,128)(2,1)S(1)} %collective-permute-done.3.refs_1_.refs_3_), channel_id=1, source_target_pairs={{0,1},{1,0},{2,3},{3,2},{4,5},{5,4},{6,7},{7,6},{8,9},{9,8},{10,11... | collective-permute-start | bytes 1769480 | tf_op jit(solution)/shard_map/ppermute | solution.py:407
  39.3 28.3 %collective-permute-start.7 = (bf16[384,768]{1,0:T(8,128)(2,1)}, bf16[384,768]{1,0:T(8,128)(2,1)S(1)}, u32[]{:S(2)}, u32[]{:S(2)}) collective-permute-start(bf16[384,768]{1,0:T(8,128)(2,1)} %tie.1.refs_2_), channel_id=1, source_target_pairs={{0,1},{1,0},{2,3},{3,2},{4,5},{5,4},{6,7},{7,6},{8,9},{9,8},{10,11... | collective-permute-start | bytes 1769480 | tf_op jit(solution)/shard_map/ppermute | solution.py:407
  43.9 23.7 %collective-permute-start.9 = (bf16[1024,256]{1,0:T(8,128)(2,1)}, bf16[1024,256]{1,0:T(8,128)(2,1)S(1)}, u32[]{:S(2)}, u32[]{:S(2)}) collective-permute-start(bf16[1024,256]{1,0:T(8,128)(2,1)} %get-tuple-element.14.after_ref.refs_0_), channel_id=1, source_target_pairs={{0,2},{1,3},{2,4},{3,5},{4,6},{5,7},{6,0},{7,1},{8,10},{9,11},{10,... | collective-permute-start | bytes 1572872 | tf_op jit(solution)/shard_map/ppermute | solution.py:404
  45.6 21.9 %collective-permute-start.10 = (bf16[1024,256]{1,0:T(8,128)(2,1)}, bf16[1024,256]{1,0:T(8,128)(2,1)}, u32[]{:S(2)}, u32[]{:S(2)}) collective-permute-start(bf16[1024,256]{1,0:T(8,128)(2,1)} %get-tuple-element.15.refs_8_), channel_id=1, source_target_pairs={{0,6},{1,7},{2,0},{3,1},{4,2},{5,3},{6,4},{7,5},{8,14},{9,15},{10,... | collective-permute-start | bytes 1572872 | tf_op jit(solution)/shard_map/ppermute | solution.py:404
  48.5 19.1 %all-to-all-start = ((bf16[8,2,128,128]{3,2,1,0:T(8,128)(2,1)}), bf16[8,2,128,128]{3,2,1,0:T(8,128)(2,1)S(1)}, u32[]{:S(2)}, u32[]{:S(2)}) async-start(bf16[8,2,128,128]{3,2,1,0:T(8,128)(2,1)} %bitcast.8), calls=%async_computation | async-start | bytes 1048576 | tf_op jit(solution)/shard_map/all_to_all | solution.py:423
  54.8 27.7 %collective-permute-start.12 = (bf16[1024,256]{1,0:T(8,128)(2,1)S(1)}, bf16[1024,256]{1,0:T(8,128)(2,1)}, u32[]{:S(2)}, u32[]{:S(2)}) collective-permute-start(bf16[1024,256]{1,0:T(8,128)(2,1)S(1)} %copy-done.14), channel_id=1, source_target_pairs={{0,6},{1,7},{2,0},{3,1},{4,2},{5,3},{6,4},{7,5},{8,14},{9,15},{10,... | collective-permute-start | bytes 1572872 | tf_op jit(solution)/shard_map/ppermute | solution.py:404
  57.4 26.5 %collective-permute-start.17 = (bf16[1024,256]{1,0:T(8,128)(2,1)}, bf16[1024,256]{1,0:T(8,128)(2,1)}, u32[]{:S(2)}, u32[]{:S(2)}) collective-permute-start(bf16[1024,256]{1,0:T(8,128)(2,1)} %get-tuple-element.15.refs_8_), channel_id=1, source_target_pairs={{0,2},{1,3},{2,4},{3,5},{4,6},{5,7},{6,0},{7,1},{8,10},{9,11},{10,... | collective-permute-start | bytes 1572872 | tf_op jit(solution)/shard_map/ppermute | solution.py:404
  75.1 25.3 %all-to-all-start.2 = ((bf16[16,2,3,48,128]{4,3,2,1,0:T(8,128)(2,1)}), bf16[16,2,3,48,128]{4,3,2,1,0:T(8,128)(2,1)}, u32[]{:S(2)}, u32[]{:S(2)}) async-start(bf16[16,2,3,48,128]{4,3,2,1,0:T(8,128)(2,1)} %get-tuple-element.16), calls=%async_computation.2 | async-start | bytes 2359296 | tf_op jit(solution)/shard_map/all_to_all | solution.py:437
  79.7 43.2 %copy-start.29 = (s32[128]{0:T(128)S(1)}, s32[128]{0:T(128)}, u32[]{:S(2)}) copy-start(s32[128]{0:T(128)} %param.19) | copy-start | bytes 1540
  79.7 52.4 %copy-start.1 = (bf16[768,768]{1,0:T(8,128)(2,1)S(1)}, bf16[768,768]{1,0:T(8,128)(2,1)}, u32[]{:S(2)}) copy-start(bf16[768,768]{1,0:T(8,128)(2,1)} %out_proj_ref.3) | copy-start | bytes 3538948
  79.7 52.4 %copy-start.2 = (f32[2,128,768]{2,1,0:T(8,128)S(1)}, f32[2,128,768]{2,1,0:T(8,128)}, u32[]{:S(2)}) copy-start(f32[2,128,768]{2,1,0:T(8,128)} %get-tuple-element.18.single_ref) | copy-start | bytes 2359300
  79.7 52.4 %copy-start.3 = (bf16[16,2,48,128]{3,2,1,0:T(8,128)(2,1)S(1)}, bf16[16,2,48,128]{3,2,1,0:T(8,128)(2,1)}, u32[]{:S(2)}) copy-start(bf16[16,2,48,128]{3,2,1,0:T(8,128)(2,1)} %get-tuple-element.17.gate_ref) | copy-start | bytes 1179652
  79.8 52.4 %copy-start.4 = (bf16[768,128]{1,0:T(8,128)(2,1)S(1)}, bf16[768,128]{1,0:T(8,128)(2,1)}, u32[]{:S(2)}) copy-start(bf16[768,128]{1,0:T(8,128)(2,1)} %return_ref.1) | copy-start | bytes 589828
  79.8 5.2 %collective-permute-start.13 = (bf16[1024,256]{1,0:T(8,128)(2,1)S(1)}, bf16[1024,256]{1,0:T(8,128)(2,1)S(1)}, u32[]{:S(2)}, u32[]{:S(2)}) collective-permute-start(bf16[1024,256]{1,0:T(8,128)(2,1)S(1)} %copy-done.14), channel_id=1, source_target_pairs={{0,1},{1,0},{2,3},{3,2},{4,5},{5,4},{6,7},{7,6},{8,9},{9,8},{10,11... | collective-permute-start | bytes 1572872 | tf_op jit(solution)/shard_map/ppermute | solution.py:407
  81.2 4.6 %collective-permute-start.19 = (bf16[1024,256]{1,0:T(8,128)(2,1)}, bf16[1024,256]{1,0:T(8,128)(2,1)}, u32[]{:S(2)}, u32[]{:S(2)}) collective-permute-start(bf16[1024,256]{1,0:T(8,128)(2,1)} %get-tuple-element.15.refs_8_), channel_id=1, source_target_pairs={{0,1},{1,0},{2,3},{3,2},{4,5},{5,4},{6,7},{7,6},{8,9},{9,8},{10,11... | collective-permute-start | bytes 1572872 | tf_op jit(solution)/shard_map/ppermute | solution.py:407
  81.3 14.6 %collective-permute-start.11 = (bf16[1024,256]{1,0:T(8,128)(2,1)}, bf16[1024,256]{1,0:T(8,128)(2,1)S(1)}, u32[]{:S(2)}, u32[]{:S(2)}) collective-permute-start(bf16[1024,256]{1,0:T(8,128)(2,1)} %copy-done.19), channel_id=1, source_target_pairs={{0,2},{1,3},{2,4},{3,5},{4,6},{5,7},{6,0},{7,1},{8,10},{9,11},{10,... | collective-permute-start | bytes 1572872 | tf_op jit(solution)/shard_map/ppermute | solution.py:404
  82.4 14.6 %collective-permute-start.18 = (bf16[1024,256]{1,0:T(8,128)(2,1)}, bf16[1024,256]{1,0:T(8,128)(2,1)S(1)}, u32[]{:S(2)}, u32[]{:S(2)}) collective-permute-start(bf16[1024,256]{1,0:T(8,128)(2,1)} %collective-permute-done.10.refs_9_.refs_11_), channel_id=1, source_target_pairs={{0,6},{1,7},{2,0},{3,1},{4,2},{5,3},{6,4},{7,5},{8,14},{9,15},{10,... | collective-permute-start | bytes 1572872 | tf_op jit(solution)/shard_map/ppermute | solution.py:404
  83.9 13.9 %collective-permute-start.14 = (bf16[1024,256]{1,0:T(8,128)(2,1)}, bf16[1024,256]{1,0:T(8,128)(2,1)S(1)}, u32[]{:S(2)}, u32[]{:S(2)}) collective-permute-start(bf16[1024,256]{1,0:T(8,128)(2,1)} %copy-done.19), channel_id=1, source_target_pairs={{0,1},{1,0},{2,3},{3,2},{4,5},{5,4},{6,7},{7,6},{8,9},{9,8},{10,11... | collective-permute-start | bytes 1572872 | tf_op jit(solution)/shard_map/ppermute | solution.py:407
  85.7 12.2 %collective-permute-start.22 = (bf16[1024,256]{1,0:T(8,128)(2,1)}, bf16[1024,256]{1,0:T(8,128)(2,1)S(1)}, u32[]{:S(2)}, u32[]{:S(2)}) collective-permute-start(bf16[1024,256]{1,0:T(8,128)(2,1)} %collective-permute-done.10.refs_9_.refs_11_), channel_id=1, source_target_pairs={{0,1},{1,0},{2,3},{3,2},{4,5},{5,4},{6,7},{7,6},{8,9},{9,8},{10,11... | collective-permute-start | bytes 1572872 | tf_op jit(solution)/shard_map/ppermute | solution.py:407
  85.7 12.2 %collective-permute-start.16 = (bf16[1024,256]{1,0:T(8,128)(2,1)}, bf16[1024,256]{1,0:T(8,128)(2,1)S(1)}, u32[]{:S(2)}, u32[]{:S(2)}) collective-permute-start(bf16[1024,256]{1,0:T(8,128)(2,1)} %collective-permute-done.12.refs_3_), channel_id=1, source_target_pairs={{0,1},{1,0},{2,3},{3,2},{4,5},{5,4},{6,7},{7,6},{8,9},{9,8},{10,11... | collective-permute-start | bytes 1572872 | tf_op jit(solution)/shard_map/ppermute | solution.py:407
  95.9 2.9 %collective-permute-start.20 = (bf16[1024,256]{1,0:T(8,128)(2,1)}, bf16[1024,256]{1,0:T(8,128)(2,1)S(1)}, u32[]{:S(2)}, u32[]{:S(2)}) collective-permute-start(bf16[1024,256]{1,0:T(8,128)(2,1)} %collective-permute-done.17.refs_9_), channel_id=1, source_target_pairs={{0,1},{1,0},{2,3},{3,2},{4,5},{5,4},{6,7},{7,6},{8,9},{9,8},{10,11... | collective-permute-start | bytes 1572872 | tf_op jit(solution)/shard_map/ppermute | solution.py:407
  97.0 2.3 %collective-permute-start.15 = (bf16[1024,256]{1,0:T(8,128)(2,1)S(1)}, bf16[1024,256]{1,0:T(8,128)(2,1)S(1)}, u32[]{:S(2)}, u32[]{:S(2)}) collective-permute-start(bf16[1024,256]{1,0:T(8,128)(2,1)S(1)} %collective-permute-done.11.refs_2_), channel_id=1, source_target_pairs={{0,1},{1,0},{2,3},{3,2},{4,5},{5,4},{6,7},{7,6},{8,9},{9,8},{10,11... | collective-permute-start | bytes 1572872 | tf_op jit(solution)/shard_map/ppermute | solution.py:407
  97.8 2.6 %collective-permute-start.21 = (bf16[1024,256]{1,0:T(8,128)(2,1)S(1)}, bf16[1024,256]{1,0:T(8,128)(2,1)}, u32[]{:S(2)}, u32[]{:S(2)}) collective-permute-start(bf16[1024,256]{1,0:T(8,128)(2,1)S(1)} %collective-permute-done.18.refs_10_), channel_id=1, source_target_pairs={{0,1},{1,0},{2,3},{3,2},{4,5},{5,4},{6,7},{7,6},{8,9},{9,8},{10,11... | collective-permute-start | bytes 1572872 | tf_op jit(solution)/shard_map/ppermute | solution.py:407
  116.0 16.1 %all-to-all-start.3 = ((bf16[16,2,48,128]{3,2,1,0:T(8,128)(2,1)}), bf16[16,2,48,128]{3,2,1,0:T(8,128)(2,1)S(1)}, u32[]{:S(2)}, u32[]{:S(2)}) async-start(bf16[16,2,48,128]{3,2,1,0:T(8,128)(2,1)} %token_attention.1), calls=%async_computation.3 | async-start | bytes 786432 | tf_op jit(solution)/shard_map/all_to_all | solution.py:441
  (25 other events, 184.7 us)

commit v2 on v1

--- a/solution.py
+++ b/solution.py
@@ -429,7 +429,7 @@
     pieces += [(slot + chips, first, across(array)) for slot, first, array in pieces]
     back_upper, ahead_lower = along(upper, 1), along(lower, -1)
     qkv, gate, single = pool_and_project(
-        place, mine, token_count, pool_proj, token_gain, pieces, heads, (back_upper, ahead_lower)
+        place, mine, token_count, pool_proj, token_gain, pieces, heads, ()
     )
     back_lower, ahead_upper = along(lower, 1), along(upper, -1)
     uppers = [upper, back_upper, along(back_upper, 1), ahead_upper]

time: 150 us -> 147 us (0.980)
  starting transfers between devices: 55.9 us -> 53 us
    all_to_all x1, waiting for transfers between devices: 10.1 us -> 2.9 us  [shards(): lax.all_to_all(mid.reshape(peers, samples // peers, atoms, channels), 'co...]
    ppermute x9, waiting for transfers between devices: 9.67 us -> 16.3 us  [along(): return lax.ppermute(value, 'col', pairs)]
    all_to_all x1, starting transfers between devices: 6.84 us -> 3.56 us  [shards(): lax.all_to_all(mixed, 'seq', split_axis=0, concat_axis=0, tiled=True)]
    ppermute x9, starting transfers between devices: 15.7 us -> 12.7 us  [along(): return lax.ppermute(value, 'col', pairs)]
    all_to_all x1, starting transfers between devices: 3.84 us -> 6.29 us  [shards(): lax.all_to_all(mid.reshape(peers, samples // peers, atoms, channels), 'co...]
    unnamed x60 -> x58, local copies, waits for them, and re-layouts: 3.67 us -> 3.55 us
  transfers between devices with their start and end apart: 27 -> 27, of which waited for: 5 -> 6; matrix products, arithmetic and copies ran while one was open for 6% -> 7% of each run, Pallas kernels for 11% -> 11%
where the time goes in v2:
time: 147 us; the launch traced here: 146 us
  starting transfers between devices  53 us (36%)
  Pallas kernels  35.2 us (24%)
  waiting for transfers between devices  29.8 us (20%)
  blocking collectives  14.4 us (10%)
  local copies, waits for them, and re-layouts  6.4 us (4%)
  matrix products  5.66 us (4%)
    ppermute x9, waiting for transfers between devices, along(): return lax.ppermute(value, 'col', pairs)  16.3 us
    pallas_call x1, Pallas kernels, token_attention(): pl.pallas_call(attend_kernel, grid=(keys // tile,), in_specs=[pl.BlockSpe...  15.6 us
    all_gather x1, blocking collectives, shards(): back = lax.all_gather(back, 'col', axis=0, tiled=True)  14.4 us
    ppermute x12, starting transfers between devices, across(): return lax.ppermute(value, 'col', [(i, i ^ 1) for i in range(peers)])  12.8 us
    ppermute x9, starting transfers between devices, along(): return lax.ppermute(value, 'col', pairs)  12.7 us
    all_to_all x1, waiting for transfers between devices, shards(): lax.all_to_all(mixed, 'seq', split_axis=0, concat_axis=0, tiled=True)  9.15 us
    pallas_call x1, Pallas kernels, atom_attention(): pl.pallas_call(functools.partial(atom_kernel, limit_atoms=limit), grid=(s...  8.01 us
    all_to_all x1, starting transfers between devices, shards(): lax.all_to_all(tile_bias, 'seq', split_axis=0, concat_axis=0, tiled=True)  7.93 us
  transfers between devices with their start and end apart: 27, of which 6 were waited for; matrix products, arithmetic and copies ran while one was open for 7% of the time, Pallas kernels for 11%

profile of v2, /device:TPU:1, one launch (start us, length us, event | category | flops | bytes accessed | tf_op | source)
XLA Modules:
  0.0 145.9 jit_solution(6661816619989547749)
XLA Ops:
  0.0 2.0 %collective-permute-start.2 = (bf16[384,768]{1,0:T(8,128)(2,1)}, bf16[384,768]{1,0:T(8,128)(2,1)S(1)}, u32[]{:S(2)}, u32[]{:S(2)}) collective-permute-start(bf16[384,768]{1,0:T(8,128)(2,1)} %bitcast.20), channel_id=1, source_target_pairs={{0,2},{1,3},{2,4},{3,5},{4,6},{5,7},{6,0},{7,1},{8,10},{9,11},{10,... | collective-permute-start | bytes 1769480 | tf_op jit(solution)/shard_map/ppermute | solution.py:404
  2.0 1.3 collective-permute-start.3
  3.4 3.1 %collective-permute-start = (bf16[16,128,128]{2,1,0:T(8,128)(2,1)}, bf16[16,128,128]{2,1,0:T(8,128)(2,1)S(1)}, u32[]{:S(2)}, u32[]{:S(2)}) collective-permute-start(bf16[16,128,128]{2,1,0:T(8,128)(2,1)} %feats_ref.1), channel_id=1, source_target_pairs={{0,1},{1,2},{2,3},{3,4},{4,5},{5,6},{6,7},{7,8},{8,9},{9,10},{10,1... | collective-permute-start | bytes 1572872 | tf_op jit(solution)/shard_map/ppermute | solution.py:395
  6.5 1.9 %collective-permute-start.1 = (bf16[16,128,128]{2,1,0:T(8,128)(2,1)}, bf16[16,128,128]{2,1,0:T(8,128)(2,1)S(1)}, u32[]{:S(2)}, u32[]{:S(2)}) collective-permute-start(bf16[16,128,128]{2,1,0:T(8,128)(2,1)} %feats_ref.1), channel_id=1, source_target_pairs={{1,0},{2,1},{3,2},{4,3},{5,4},{6,5},{7,6},{8,7},{9,8},{10,9},{11,1... | collective-permute-start | bytes 1572872 | tf_op jit(solution)/shard_map/ppermute | solution.py:396
  8.5 5.7 %multiply_convert_fusion = bf16[16,128,256]{2,0,1:T(8,128)(2,1)S(1)} fusion(bf16[128,256,128]{2,1,0:T(8,128)(2,1)} %param.28, bf16[128,16]{0,1:T(8,128)(2,1)S(1)} %copy-done), kind=kOutput, calls=%fused_computation | convolution fusion | flops 135266304 | bytes 9441280 | tf_op jit(solution)/shard_map/ijc,ch->hij/dot_general | solution.py:412
  14.2 1.3 copy.27
  15.6 7.9 %all-to-all-start.1 = ((bf16[16,128,256]{2,1,0:T(8,128)(2,1)}), bf16[16,128,256]{2,1,0:T(8,128)(2,1)}, u32[]{:S(2)}, u32[]{:S(2)}) async-start(bf16[16,128,256]{2,1,0:T(8,128)(2,1)} %copy.27), calls=%async_computation.1 | async-start | bytes 2097152 | tf_op jit(solution)/shard_map/all_to_all | solution.py:414
  23.5 2.4 %collective-permute-start.4 = (bf16[384,768]{1,0:T(8,128)(2,1)}, bf16[384,768]{1,0:T(8,128)(2,1)}, u32[]{:S(2)}, u32[]{:S(2)}) collective-permute-start(bf16[384,768]{1,0:T(8,128)(2,1)} %bitcast.22), channel_id=1, source_target_pairs={{0,4},{1,5},{2,6},{3,7},{4,0},{5,1},{6,2},{7,3},{8,12},{9,13},{10,... | collective-permute-start | bytes 1769480 | tf_op jit(solution)/shard_map/ppermute | solution.py:404
  26.0 1.8 %collective-permute-start.5 = (bf16[384,768]{1,0:T(8,128)(2,1)}, bf16[384,768]{1,0:T(8,128)(2,1)}, u32[]{:S(2)}, u32[]{:S(2)}) collective-permute-start(bf16[384,768]{1,0:T(8,128)(2,1)} %bitcast.23), channel_id=1, source_target_pairs={{0,1},{1,0},{2,3},{3,2},{4,5},{5,4},{6,7},{7,6},{8,9},{9,8},{10,11... | collective-permute-start | bytes 1769480 | tf_op jit(solution)/shard_map/ppermute | solution.py:407
  28.4 8.0 %atom_attention.1 = (bf16[16,128,128]{2,1,0:T(8,128)(2,1)}, f32[8,128]{1,0:T(8,128)S(1)}) custom-call(s32[4]{0:T(128)S(1)} %copy-done.12, s32[1]{0:T(128)} %bitcast.3.off_ref, f32[16,4]{1,0:T(8,128)S(1)} %copy.26.wpair_ref, bf16[16,128,128]{2,1,0:T(8,128)(2,1)S(1)} %copy-done.8, bf16[16,128,128]{2,1,0:T(8,128)(2,1)S(1)} %collective-permute-done.before_ref, ...), custom_call_target="tpu_custom_call" | custom-call | flops 8000000000 | bytes 3000000 | tf_op jit(solution)/shard_map/atom_attention/pallas_call | solution.py:112
  37.0 2.3 %split_rows.1 = (bf16[1024,256]{1,0:T(8,128)(2,1)}, bf16[1024,256]{1,0:T(8,128)(2,1)}) custom-call(bf16[2048,256]{1,0:T(8,128)(2,1)} %bitcast.12.value_ref, f32[8,128]{1,0:T(8,128)} %copy-done.5), custom_call_target="tpu_custom_call" | custom-call | bytes 2097152 | tf_op jit(solution)/shard_map/split_rows/pallas_call | solution.py:154
  39.3 4.6 %collective-permute-start.7 = (bf16[384,768]{1,0:T(8,128)(2,1)}, bf16[384,768]{1,0:T(8,128)(2,1)S(1)}, u32[]{:S(2)}, u32[]{:S(2)}) collective-permute-start(bf16[384,768]{1,0:T(8,128)(2,1)} %tie.1.refs_2_), channel_id=1, source_target_pairs={{0,1},{1,0},{2,3},{3,2},{4,5},{5,4},{6,7},{7,6},{8,9},{9,8},{10,11... | collective-permute-start | bytes 1769480 | tf_op jit(solution)/shard_map/ppermute | solution.py:407
  43.9 6.3 %all-to-all-start = ((bf16[8,2,128,128]{3,2,1,0:T(8,128)(2,1)}), bf16[8,2,128,128]{3,2,1,0:T(8,128)(2,1)S(1)}, u32[]{:S(2)}, u32[]{:S(2)}) async-start(bf16[8,2,128,128]{3,2,1,0:T(8,128)(2,1)} %bitcast.8), calls=%async_computation | async-start | bytes 1048576 | tf_op jit(solution)/shard_map/all_to_all | solution.py:423
  52.7 1.4 collective-permute-start.9
  54.0 1.3 collective-permute-start.11
  55.3 1.4 collective-permute-start.17
  56.8 2.9 %all-to-all-done.mid_ref = bf16[8,2,128,128]{3,2,1,0:T(8,128)(2,1)S(1)} async-done(((bf16[8,2,128,128]{3,2,1,0:T(8,128)(2,1)}), bf16[8,2,128,128]{3,2,1,0:T(8,128)(2,1)S(1)}, u32[]{:S(2)}, u32[]{:S(2)}) %all-to-all-start) | async-done | bytes 524320 | tf_op jit(solution)/shard_map/all_to_all | solution.py:423
  60.7 6.4 %pool_and_project.1 = (bf16[16,2,3,48,128]{4,3,2,1,0:T(8,128)(2,1)}, bf16[16,2,48,128]{3,2,1,0:T(8,128)(2,1)}, f32[2,128,768]{2,1,0:T(8,128)}) custom-call(s32[2]{0:T(128)} %pad_add_fusion.place_ref, bf16[8,2,128,128]{3,2,1,0:T(8,128)(2,1)} %copy-done.15, f32[1,128]{1,0:T(1,128)} %get-tuple-element.20.count_row_ref, f32[128,1]{1,0:T(8,128)} %copy.28.count_col_ref, ...), custom_call_target="tpu_custom_call" | custom-call | flops 6000000000 | bytes 8000000 | tf_op jit(solution)/shard_map/pool_and_project/pallas_call | solution.py:234
  67.1 4.6 %all-to-all-start.2 = ((bf16[16,2,3,48,128]{4,3,2,1,0:T(8,128)(2,1)}), bf16[16,2,3,48,128]{4,3,2,1,0:T(8,128)(2,1)}, u32[]{:S(2)}, u32[]{:S(2)}) async-start(bf16[16,2,3,48,128]{4,3,2,1,0:T(8,128)(2,1)} %get-tuple-element.15), calls=%async_computation.2 | async-start | bytes 2359296 | tf_op jit(solution)/shard_map/all_to_all | solution.py:437
  71.7 1.4 collective-permute-start.12
  73.3 7.5 %collective-permute-done.17.refs_11_ = bf16[1024,256]{1,0:T(8,128)(2,1)} collective-permute-done((bf16[1024,256]{1,0:T(8,128)(2,1)}, bf16[1024,256]{1,0:T(8,128)(2,1)}, u32[]{:S(2)}, u32[]{:S(2)}) %collective-permute-start.17) | collective-permute-done | bytes 524320 | tf_op jit(solution)/shard_map/ppermute | solution.py:404
  80.7 1.4 collective-permute-start.10
  82.1 1.4 collective-permute-start.18
  83.5 1.3 collective-permute-start.13
  86.2 8.8 %collective-permute-done.10.refs_2_ = bf16[1024,256]{1,0:T(8,128)(2,1)S(1)} collective-permute-done((bf16[1024,256]{1,0:T(8,128)(2,1)}, bf16[1024,256]{1,0:T(8,128)(2,1)S(1)}, u32[]{:S(2)}, u32[]{:S(2)}) %collective-permute-start.10) | collective-permute-done | bytes 524320 | tf_op jit(solution)/shard_map/ppermute | solution.py:404
  95.0 1.6 %collective-permute-start.20 = (bf16[1024,256]{1,0:T(8,128)(2,1)}, bf16[1024,256]{1,0:T(8,128)(2,1)S(1)}, u32[]{:S(2)}, u32[]{:S(2)}) collective-permute-start(bf16[1024,256]{1,0:T(8,128)(2,1)} %collective-permute-done.16.refs_9_), channel_id=1, source_target_pairs={{0,1},{1,0},{2,3},{3,2},{4,5},{5,4},{6,7},{7,6},{8,9},{9,8},{10,11... | collective-permute-start | bytes 1572872 | tf_op jit(solution)/shard_map/ppermute | solution.py:407
  99.2 0.8 copy-done.26
  100.0 15.6 %token_attention.1 = bf16[16,2,48,128]{3,2,1,0:T(8,128)(2,1)} custom-call(s32[2]{0:T(128)} %pad_add_fusion.place_ref, bf16[16,2,3,48,128]{4,3,2,1,0:T(8,128)(2,1)} %all-to-all-done.2.qkv_ref, bf16[1024,256]{1,0:T(8,128)(2,1)} %get-tuple-element.14.after_ref.refs_0_, bf16[1024,256]{1,0:T(8,128)(2,1)} %collective-permute-done.9.refs_1_, ...), custom_call_target="tpu_custom_call" | custom-call | flops 4294967296 | bytes 9568256 | tf_op jit(solution)/shard_map/token_attention/pallas_call | solution.py:316
  115.7 3.6 %all-to-all-start.3 = ((bf16[16,2,48,128]{3,2,1,0:T(8,128)(2,1)}), bf16[16,2,48,128]{3,2,1,0:T(8,128)(2,1)S(1)}, u32[]{:S(2)}, u32[]{:S(2)}) async-start(bf16[16,2,48,128]{3,2,1,0:T(8,128)(2,1)} %token_attention.1), calls=%async_computation.3 | async-start | bytes 786432 | tf_op jit(solution)/shard_map/all_to_all | solution.py:441
  119.4 9.2 %all-to-all-done.3.mixed_ref = bf16[16,2,48,128]{3,2,1,0:T(8,128)(2,1)S(1)} async-done(((bf16[16,2,48,128]{3,2,1,0:T(8,128)(2,1)}), bf16[16,2,48,128]{3,2,1,0:T(8,128)(2,1)S(1)}, u32[]{:S(2)}, u32[]{:S(2)}) %all-to-all-start.3) | async-done | bytes 393248 | tf_op jit(solution)/shard_map/all_to_all | solution.py:441
  129.4 14.4 %all_gather.3.back_ref = bf16[16,128,128]{2,1,0:T(8,128)(2,1)S(1)} all-gather(bf16[2,128,128]{2,1,0:T(8,128)(2,1)S(1)} %out_project.1), channel_id=1, replica_groups=mesh['seq'=16,'col'=8] {'col'}, dimensions={0}, use_global_device_ids=true | all-gather | bytes 589824 | tf_op jit(solution)/shard_map/all_gather | solution.py:443
  143.7 2.2 %spread_back.1 = bf16[16,128,128]{2,1,0:T(8,128)(2,1)} custom-call(s32[128,1]{1,0:T(8,128)S(1)} %copy.29.tok_ref, bf16[16,128,128]{2,1,0:T(8,128)(2,1)S(1)} %all_gather.3.back_ref, bf16[16,128,128]{2,1,0:T(8,128)(2,1)} %get-tuple-element.12.mid_ref), custom_call_target="tpu_custom_call" | custom-call | flops 100000000 | bytes 2000000 | tf_op jit(solution)/shard_map/spread_back/pallas_call | solution.py:369
  (97 shorter events, 9.7 us)
Async XLA Ops:
  0.0 27.9 %collective-permute-start.2 = (bf16[384,768]{1,0:T(8,128)(2,1)}, bf16[384,768]{1,0:T(8,128)(2,1)S(1)}, u32[]{:S(2)}, u32[]{:S(2)}) collective-permute-start(bf16[384,768]{1,0:T(8,128)(2,1)} %bitcast.20), channel_id=1, source_target_pairs={{0,2},{1,3},{2,4},{3,5},{4,6},{5,7},{6,0},{7,1},{8,10},{9,11},{10,... | collective-permute-start | bytes 1769480 | tf_op jit(solution)/shard_map/ppermute | solution.py:404
  2.0 25.9 %collective-permute-start.3 = (bf16[384,768]{1,0:T(8,128)(2,1)}, bf16[384,768]{1,0:T(8,128)(2,1)S(1)}, u32[]{:S(2)}, u32[]{:S(2)}) collective-permute-start(bf16[384,768]{1,0:T(8,128)(2,1)} %bitcast.21), channel_id=1, source_target_pairs={{0,6},{1,7},{2,0},{3,1},{4,2},{5,3},{6,4},{7,5},{8,14},{9,15},{10,... | collective-permute-start | bytes 1769480 | tf_op jit(solution)/shard_map/ppermute | solution.py:404
  3.4 22.6 %collective-permute-start = (bf16[16,128,128]{2,1,0:T(8,128)(2,1)}, bf16[16,128,128]{2,1,0:T(8,128)(2,1)S(1)}, u32[]{:S(2)}, u32[]{:S(2)}) collective-permute-start(bf16[16,128,128]{2,1,0:T(8,128)(2,1)} %feats_ref.1), channel_id=1, source_target_pairs={{0,1},{1,2},{2,3},{3,4},{4,5},{5,6},{6,7},{7,8},{8,9},{9,10},{10,1... | collective-permute-start | bytes 1572872 | tf_op jit(solution)/shard_map/ppermute | solution.py:395
  6.5 21.8 %collective-permute-start.1 = (bf16[16,128,128]{2,1,0:T(8,128)(2,1)}, bf16[16,128,128]{2,1,0:T(8,128)(2,1)S(1)}, u32[]{:S(2)}, u32[]{:S(2)}) collective-permute-start(bf16[16,128,128]{2,1,0:T(8,128)(2,1)} %feats_ref.1), channel_id=1, source_target_pairs={{1,0},{2,1},{3,2},{4,3},{5,4},{6,5},{7,6},{8,7},{9,8},{10,9},{11,1... | collective-permute-start | bytes 1572872 | tf_op jit(solution)/shard_map/ppermute | solution.py:396
  15.6 21.5 %all-to-all-start.1 = ((bf16[16,128,256]{2,1,0:T(8,128)(2,1)}), bf16[16,128,256]{2,1,0:T(8,128)(2,1)}, u32[]{:S(2)}, u32[]{:S(2)}) async-start(bf16[16,128,256]{2,1,0:T(8,128)(2,1)} %copy.27), calls=%async_computation.1 | async-start | bytes 2097152 | tf_op jit(solution)/shard_map/all_to_all | solution.py:414
  23.5 15.8 %collective-permute-start.4 = (bf16[384,768]{1,0:T(8,128)(2,1)}, bf16[384,768]{1,0:T(8,128)(2,1)}, u32[]{:S(2)}, u32[]{:S(2)}) collective-permute-start(bf16[384,768]{1,0:T(8,128)(2,1)} %bitcast.22), channel_id=1, source_target_pairs={{0,4},{1,5},{2,6},{3,7},{4,0},{5,1},{6,2},{7,3},{8,12},{9,13},{10,... | collective-permute-start | bytes 1769480 | tf_op jit(solution)/shard_map/ppermute | solution.py:404
  26.0 28.0 %collective-permute-start.5 = (bf16[384,768]{1,0:T(8,128)(2,1)}, bf16[384,768]{1,0:T(8,128)(2,1)}, u32[]{:S(2)}, u32[]{:S(2)}) collective-permute-start(bf16[384,768]{1,0:T(8,128)(2,1)} %bitcast.23), channel_id=1, source_target_pairs={{0,1},{1,0},{2,3},{3,2},{4,5},{5,4},{6,7},{7,6},{8,9},{9,8},{10,11... | collective-permute-start | bytes 1769480 | tf_op jit(solution)/shard_map/ppermute | solution.py:407
  27.9 27.5 %collective-permute-start.6 = (bf16[384,768]{1,0:T(8,128)(2,1)S(1)}, bf16[384,768]{1,0:T(8,128)(2,1)}, u32[]{:S(2)}, u32[]{:S(2)}) collective-permute-start(bf16[384,768]{1,0:T(8,128)(2,1)S(1)} %collective-permute-done.2.refs_0_.refs_1_), channel_id=1, source_target_pairs={{0,1},{1,0},{2,3},{3,2},{4,5},{5,4},{6,7},{7,6},{8,9},{9,8},{10,11... | collective-permute-start | bytes 1769480 | tf_op jit(solution)/shard_map/ppermute | solution.py:407
  28.0 28.8 %collective-permute-start.8 = (bf16[384,768]{1,0:T(8,128)(2,1)S(1)}, bf16[384,768]{1,0:T(8,128)(2,1)}, u32[]{:S(2)}, u32[]{:S(2)}) collective-permute-start(bf16[384,768]{1,0:T(8,128)(2,1)S(1)} %collective-permute-done.3.refs_1_.refs_3_), channel_id=1, source_target_pairs={{0,1},{1,0},{2,3},{3,2},{4,5},{5,4},{6,7},{7,6},{8,9},{9,8},{10,11... | collective-permute-start | bytes 1769480 | tf_op jit(solution)/shard_map/ppermute | solution.py:407
  39.3 20.4 %collective-permute-start.7 = (bf16[384,768]{1,0:T(8,128)(2,1)}, bf16[384,768]{1,0:T(8,128)(2,1)S(1)}, u32[]{:S(2)}, u32[]{:S(2)}) collective-permute-start(bf16[384,768]{1,0:T(8,128)(2,1)} %tie.1.refs_2_), channel_id=1, source_target_pairs={{0,1},{1,0},{2,3},{3,2},{4,5},{5,4},{6,7},{7,6},{8,9},{9,8},{10,11... | collective-permute-start | bytes 1769480 | tf_op jit(solution)/shard_map/ppermute | solution.py:407
  43.9 15.8 %all-to-all-start = ((bf16[8,2,128,128]{3,2,1,0:T(8,128)(2,1)}), bf16[8,2,128,128]{3,2,1,0:T(8,128)(2,1)S(1)}, u32[]{:S(2)}, u32[]{:S(2)}) async-start(bf16[8,2,128,128]{3,2,1,0:T(8,128)(2,1)} %bitcast.8), calls=%async_computation | async-start | bytes 1048576 | tf_op jit(solution)/shard_map/all_to_all | solution.py:423
  52.7 20.5 %collective-permute-start.9 = (bf16[1024,256]{1,0:T(8,128)(2,1)S(1)}, bf16[1024,256]{1,0:T(8,128)(2,1)}, u32[]{:S(2)}, u32[]{:S(2)}) collective-permute-start(bf16[1024,256]{1,0:T(8,128)(2,1)S(1)} %copy-done.14), channel_id=1, source_target_pairs={{0,2},{1,3},{2,4},{3,5},{4,6},{5,7},{6,0},{7,1},{8,10},{9,11},{10,... | collective-permute-start | bytes 1572872 | tf_op jit(solution)/shard_map/ppermute | solution.py:404
  54.0 28.1 %collective-permute-start.11 = (bf16[1024,256]{1,0:T(8,128)(2,1)S(1)}, bf16[1024,256]{1,0:T(8,128)(2,1)}, u32[]{:S(2)}, u32[]{:S(2)}) collective-permute-start(bf16[1024,256]{1,0:T(8,128)(2,1)S(1)} %copy-done.14), channel_id=1, source_target_pairs={{0,6},{1,7},{2,0},{3,1},{4,2},{5,3},{6,4},{7,5},{8,14},{9,15},{10,... | collective-permute-start | bytes 1572872 | tf_op jit(solution)/shard_map/ppermute | solution.py:404
  55.3 25.4 %collective-permute-start.17 = (bf16[1024,256]{1,0:T(8,128)(2,1)}, bf16[1024,256]{1,0:T(8,128)(2,1)}, u32[]{:S(2)}, u32[]{:S(2)}) collective-permute-start(bf16[1024,256]{1,0:T(8,128)(2,1)} %get-tuple-element.16.refs_8_), channel_id=1, source_target_pairs={{0,6},{1,7},{2,0},{3,1},{4,2},{5,3},{6,4},{7,5},{8,14},{9,15},{10,... | collective-permute-start | bytes 1572872 | tf_op jit(solution)/shard_map/ppermute | solution.py:404
  56.7 26.8 %collective-permute-start.16 = (bf16[1024,256]{1,0:T(8,128)(2,1)}, bf16[1024,256]{1,0:T(8,128)(2,1)}, u32[]{:S(2)}, u32[]{:S(2)}) collective-permute-start(bf16[1024,256]{1,0:T(8,128)(2,1)} %get-tuple-element.16.refs_8_), channel_id=1, source_target_pairs={{0,2},{1,3},{2,4},{3,5},{4,6},{5,7},{6,0},{7,1},{8,10},{9,11},{10,... | collective-permute-start | bytes 1572872 | tf_op jit(solution)/shard_map/ppermute | solution.py:404
  67.1 33.0 %all-to-all-start.2 = ((bf16[16,2,3,48,128]{4,3,2,1,0:T(8,128)(2,1)}), bf16[16,2,3,48,128]{4,3,2,1,0:T(8,128)(2,1)}, u32[]{:S(2)}, u32[]{:S(2)}) async-start(bf16[16,2,3,48,128]{4,3,2,1,0:T(8,128)(2,1)} %get-tuple-element.15), calls=%async_computation.2 | async-start | bytes 2359296 | tf_op jit(solution)/shard_map/all_to_all | solution.py:437
  71.7 47.6 %copy-start.28 = (s32[128]{0:T(128)S(1)}, s32[128]{0:T(128)}, u32[]{:S(2)}) copy-start(s32[128]{0:T(128)} %param.19) | copy-start | bytes 1540
  71.7 56.9 %copy-start.1 = (bf16[768,768]{1,0:T(8,128)(2,1)S(1)}, bf16[768,768]{1,0:T(8,128)(2,1)}, u32[]{:S(2)}) copy-start(bf16[768,768]{1,0:T(8,128)(2,1)} %out_proj_ref.3) | copy-start | bytes 3538948
  71.7 56.8 %copy-start.2 = (f32[2,128,768]{2,1,0:T(8,128)S(1)}, f32[2,128,768]{2,1,0:T(8,128)}, u32[]{:S(2)}) copy-start(f32[2,128,768]{2,1,0:T(8,128)} %get-tuple-element.18.single_ref) | copy-start | bytes 2359300
  71.7 56.8 %copy-start.3 = (bf16[16,2,48,128]{3,2,1,0:T(8,128)(2,1)S(1)}, bf16[16,2,48,128]{3,2,1,0:T(8,128)(2,1)}, u32[]{:S(2)}) copy-start(bf16[16,2,48,128]{3,2,1,0:T(8,128)(2,1)} %get-tuple-element.17.gate_ref) | copy-start | bytes 1179652
  71.7 56.8 %copy-start.4 = (bf16[768,128]{1,0:T(8,128)(2,1)S(1)}, bf16[768,128]{1,0:T(8,128)(2,1)}, u32[]{:S(2)}) copy-start(bf16[768,128]{1,0:T(8,128)(2,1)} %return_ref.1) | copy-start | bytes 589828
  71.7 13.1 %collective-permute-start.12 = (bf16[1024,256]{1,0:T(8,128)(2,1)S(1)}, bf16[1024,256]{1,0:T(8,128)(2,1)S(1)}, u32[]{:S(2)}, u32[]{:S(2)}) collective-permute-start(bf16[1024,256]{1,0:T(8,128)(2,1)S(1)} %copy-done.14), channel_id=1, source_target_pairs={{0,1},{1,0},{2,3},{3,2},{4,5},{5,4},{6,7},{7,6},{8,9},{9,8},{10,11... | collective-permute-start | bytes 1572872 | tf_op jit(solution)/shard_map/ppermute | solution.py:407
  73.2 12.5 %collective-permute-start.19 = (bf16[1024,256]{1,0:T(8,128)(2,1)}, bf16[1024,256]{1,0:T(8,128)(2,1)}, u32[]{:S(2)}, u32[]{:S(2)}) collective-permute-start(bf16[1024,256]{1,0:T(8,128)(2,1)} %get-tuple-element.16.refs_8_), channel_id=1, source_target_pairs={{0,1},{1,0},{2,3},{3,2},{4,5},{5,4},{6,7},{7,6},{8,9},{9,8},{10,11... | collective-permute-start | bytes 1572872 | tf_op jit(solution)/shard_map/ppermute | solution.py:407
  80.7 14.2 %collective-permute-start.10 = (bf16[1024,256]{1,0:T(8,128)(2,1)}, bf16[1024,256]{1,0:T(8,128)(2,1)S(1)}, u32[]{:S(2)}, u32[]{:S(2)}) collective-permute-start(bf16[1024,256]{1,0:T(8,128)(2,1)} %collective-permute-done.9.refs_1_), channel_id=1, source_target_pairs={{0,2},{1,3},{2,4},{3,5},{4,6},{5,7},{6,0},{7,1},{8,10},{9,11},{10,... | collective-permute-start | bytes 1572872 | tf_op jit(solution)/shard_map/ppermute | solution.py:404
  82.1 14.5 %collective-permute-start.18 = (bf16[1024,256]{1,0:T(8,128)(2,1)}, bf16[1024,256]{1,0:T(8,128)(2,1)S(1)}, u32[]{:S(2)}, u32[]{:S(2)}) collective-permute-start(bf16[1024,256]{1,0:T(8,128)(2,1)} %collective-permute-done.17.refs_11_), channel_id=1, source_target_pairs={{0,6},{1,7},{2,0},{3,1},{4,2},{5,3},{6,4},{7,5},{8,14},{9,15},{10,... | collective-permute-start | bytes 1572872 | tf_op jit(solution)/shard_map/ppermute | solution.py:404
  83.5 13.9 %collective-permute-start.13 = (bf16[1024,256]{1,0:T(8,128)(2,1)}, bf16[1024,256]{1,0:T(8,128)(2,1)S(1)}, u32[]{:S(2)}, u32[]{:S(2)}) collective-permute-start(bf16[1024,256]{1,0:T(8,128)(2,1)} %collective-permute-done.9.refs_1_), channel_id=1, source_target_pairs={{0,1},{1,0},{2,3},{3,2},{4,5},{5,4},{6,7},{7,6},{8,9},{9,8},{10,11... | collective-permute-start | bytes 1572872 | tf_op jit(solution)/shard_map/ppermute | solution.py:407
  85.7 11.9 %collective-permute-start.22 = (bf16[1024,256]{1,0:T(8,128)(2,1)}, bf16[1024,256]{1,0:T(8,128)(2,1)S(1)}, u32[]{:S(2)}, u32[]{:S(2)}) collective-permute-start(bf16[1024,256]{1,0:T(8,128)(2,1)} %collective-permute-done.17.refs_11_), channel_id=1, source_target_pairs={{0,1},{1,0},{2,3},{3,2},{4,5},{5,4},{6,7},{7,6},{8,9},{9,8},{10,11... | collective-permute-start | bytes 1572872 | tf_op jit(solution)/shard_map/ppermute | solution.py:407
  85.7 11.9 %collective-permute-start.15 = (bf16[1024,256]{1,0:T(8,128)(2,1)}, bf16[1024,256]{1,0:T(8,128)(2,1)S(1)}, u32[]{:S(2)}, u32[]{:S(2)}) collective-permute-start(bf16[1024,256]{1,0:T(8,128)(2,1)} %collective-permute-done.11.refs_3_), channel_id=1, source_target_pairs={{0,1},{1,0},{2,3},{3,2},{4,5},{5,4},{6,7},{7,6},{8,9},{9,8},{10,11... | collective-permute-start | bytes 1572872 | tf_op jit(solution)/shard_map/ppermute | solution.py:407
  95.0 3.4 %collective-permute-start.20 = (bf16[1024,256]{1,0:T(8,128)(2,1)}, bf16[1024,256]{1,0:T(8,128)(2,1)S(1)}, u32[]{:S(2)}, u32[]{:S(2)}) collective-permute-start(bf16[1024,256]{1,0:T(8,128)(2,1)} %collective-permute-done.16.refs_9_), channel_id=1, source_target_pairs={{0,1},{1,0},{2,3},{3,2},{4,5},{5,4},{6,7},{7,6},{8,9},{9,8},{10,11... | collective-permute-start | bytes 1572872 | tf_op jit(solution)/shard_map/ppermute | solution.py:407
  96.6 2.3 %collective-permute-start.14 = (bf16[1024,256]{1,0:T(8,128)(2,1)S(1)}, bf16[1024,256]{1,0:T(8,128)(2,1)S(1)}, u32[]{:S(2)}, u32[]{:S(2)}) collective-permute-start(bf16[1024,256]{1,0:T(8,128)(2,1)S(1)} %collective-permute-done.10.refs_2_), channel_id=1, source_target_pairs={{0,1},{1,0},{2,3},{3,2},{4,5},{5,4},{6,7},{7,6},{8,9},{9,8},{10,11... | collective-permute-start | bytes 1572872 | tf_op jit(solution)/shard_map/ppermute | solution.py:407
  97.4 2.6 %collective-permute-start.21 = (bf16[1024,256]{1,0:T(8,128)(2,1)S(1)}, bf16[1024,256]{1,0:T(8,128)(2,1)}, u32[]{:S(2)}, u32[]{:S(2)}) collective-permute-start(bf16[1024,256]{1,0:T(8,128)(2,1)S(1)} %collective-permute-done.18.refs_10_), channel_id=1, source_target_pairs={{0,1},{1,0},{2,3},{3,2},{4,5},{5,4},{6,7},{7,6},{8,9},{9,8},{10,11... | collective-permute-start | bytes 1572872 | tf_op jit(solution)/shard_map/ppermute | solution.py:407
  115.7 12.9 %all-to-all-start.3 = ((bf16[16,2,48,128]{3,2,1,0:T(8,128)(2,1)}), bf16[16,2,48,128]{3,2,1,0:T(8,128)(2,1)S(1)}, u32[]{:S(2)}, u32[]{:S(2)}) async-start(bf16[16,2,48,128]{3,2,1,0:T(8,128)(2,1)} %token_attention.1), calls=%async_computation.3 | async-start | bytes 786432 | tf_op jit(solution)/shard_map/all_to_all | solution.py:441
  (24 other events, 177.8 us)

commit v3 on v2

--- a/solution.py
+++ b/solution.py
@@ -429,7 +429,7 @@
     pieces += [(slot + chips, first, across(array)) for slot, first, array in pieces]
     back_upper, ahead_lower = along(upper, 1), along(lower, -1)
     qkv, gate, single = pool_and_project(
-        place, mine, token_count, pool_proj, token_gain, pieces, heads, ()
+        place, mine, token_count, pool_proj, token_gain, pieces, heads, (ahead_lower,)
     )
     back_lower, ahead_upper = along(lower, 1), along(upper, -1)
     uppers = [upper, back_upper, along(back_upper, 1), ahead_upper]

time: 147 us -> 149 us (1.014)
  starting transfers between devices: 53 us -> 55.6 us
    ppermute x9, waiting for transfers between devices: 16.3 us -> 10.5 us  [along(): return lax.ppermute(value, 'col', pairs)]
    all_to_all x1, waiting for transfers between devices: 2.9 us -> 8.15 us  [shards(): lax.all_to_all(mid.reshape(peers, samples // peers, atoms, channels), 'co...]
    ppermute x9, starting transfers between devices: 12.7 us -> 16.6 us  [along(): return lax.ppermute(value, 'col', pairs)]
    all_to_all x1, starting transfers between devices: 3.56 us -> 6.59 us  [shards(): lax.all_to_all(mixed, 'seq', split_axis=0, concat_axis=0, tiled=True)]
    all_to_all x1, starting transfers between devices: 6.29 us -> 3.74 us  [shards(): lax.all_to_all(mid.reshape(peers, samples // peers, atoms, channels), 'co...]
    ppermute x12, starting transfers between devices: 12.8 us -> 11.1 us  [across(): return lax.ppermute(value, 'col', [(i, i ^ 1) for i in range(peers)])]
    unnamed x58 -> x60, local copies, waits for them, and re-layouts: 3.55 us -> 3.87 us
  transfers between devices with their start and end apart: 27 -> 27, of which waited for: 6 -> 6; matrix products, arithmetic and copies ran while one was open for 7% -> 6% of each run, Pallas kernels for 11% -> 11%
where the time goes in v3:
time: 149 us; the launch traced here: 148 us
  starting transfers between devices  55.6 us (37%)
  Pallas kernels  35.3 us (24%)
  waiting for transfers between devices  29.2 us (20%)
  blocking collectives  14.5 us (10%)
  local copies, waits for them, and re-layouts  6.73 us (5%)
  matrix products  5.66 us (4%)
    ppermute x9, starting transfers between devices, along(): return lax.ppermute(value, 'col', pairs)  16.6 us
    pallas_call x1, Pallas kernels, token_attention(): pl.pallas_call(attend_kernel, grid=(keys // tile,), in_specs=[pl.BlockSpe...  15.6 us
    all_gather x1, blocking collectives, shards(): back = lax.all_gather(back, 'col', axis=0, tiled=True)  14.5 us
    ppermute x12, starting transfers between devices, across(): return lax.ppermute(value, 'col', [(i, i ^ 1) for i in range(peers)])  11.1 us
    ppermute x9, waiting for transfers between devices, along(): return lax.ppermute(value, 'col', pairs)  10.5 us
    all_to_all x1, waiting for transfers between devices, shards(): lax.all_to_all(mixed, 'seq', split_axis=0, concat_axis=0, tiled=True)  9.1 us
    all_to_all x1, waiting for transfers between devices, shards(): lax.all_to_all(mid.reshape(peers, samples // peers, atoms, channels), 'co...  8.15 us
    pallas_call x1, Pallas kernels, atom_attention(): pl.pallas_call(functools.partial(atom_kernel, limit_atoms=limit), grid=(s...  8.01 us
  transfers between devices with their start and end apart: 27, of which 6 were waited for; matrix products, arithmetic and copies ran while one was open for 6% of the time, Pallas kernels for 11%

profile of v3, /device:TPU:1, one launch (start us, length us, event | category | flops | bytes accessed | tf_op | source)
XLA Modules:
  0.0 148.4 jit_solution(1982144502850146545)
XLA Ops:
  0.0 2.0 %collective-permute-start.2 = (bf16[384,768]{1,0:T(8,128)(2,1)}, bf16[384,768]{1,0:T(8,128)(2,1)S(1)}, u32[]{:S(2)}, u32[]{:S(2)}) collective-permute-start(bf16[384,768]{1,0:T(8,128)(2,1)} %bitcast.20), channel_id=1, source_target_pairs={{0,2},{1,3},{2,4},{3,5},{4,6},{5,7},{6,0},{7,1},{8,10},{9,11},{10,... | collective-permute-start | bytes 1769480 | tf_op jit(solution)/shard_map/ppermute | solution.py:404
  2.0 1.3 collective-permute-start.3
  3.4 3.1 %collective-permute-start = (bf16[16,128,128]{2,1,0:T(8,128)(2,1)}, bf16[16,128,128]{2,1,0:T(8,128)(2,1)S(1)}, u32[]{:S(2)}, u32[]{:S(2)}) collective-permute-start(bf16[16,128,128]{2,1,0:T(8,128)(2,1)} %feats_ref.1), channel_id=1, source_target_pairs={{0,1},{1,2},{2,3},{3,4},{4,5},{5,6},{6,7},{7,8},{8,9},{9,10},{10,1... | collective-permute-start | bytes 1572872 | tf_op jit(solution)/shard_map/ppermute | solution.py:395
  6.5 1.9 %collective-permute-start.1 = (bf16[16,128,128]{2,1,0:T(8,128)(2,1)}, bf16[16,128,128]{2,1,0:T(8,128)(2,1)S(1)}, u32[]{:S(2)}, u32[]{:S(2)}) collective-permute-start(bf16[16,128,128]{2,1,0:T(8,128)(2,1)} %feats_ref.1), channel_id=1, source_target_pairs={{1,0},{2,1},{3,2},{4,3},{5,4},{6,5},{7,6},{8,7},{9,8},{10,9},{11,1... | collective-permute-start | bytes 1572872 | tf_op jit(solution)/shard_map/ppermute | solution.py:396
  8.5 5.7 %multiply_convert_fusion = bf16[16,128,256]{2,0,1:T(8,128)(2,1)S(1)} fusion(bf16[128,256,128]{2,1,0:T(8,128)(2,1)} %param.28, bf16[128,16]{0,1:T(8,128)(2,1)S(1)} %copy-done), kind=kOutput, calls=%fused_computation | convolution fusion | flops 135266304 | bytes 9441280 | tf_op jit(solution)/shard_map/ijc,ch->hij/dot_general | solution.py:412
  14.2 1.3 copy.27
  15.6 7.9 %all-to-all-start.1 = ((bf16[16,128,256]{2,1,0:T(8,128)(2,1)}), bf16[16,128,256]{2,1,0:T(8,128)(2,1)}, u32[]{:S(2)}, u32[]{:S(2)}) async-start(bf16[16,128,256]{2,1,0:T(8,128)(2,1)} %copy.27), calls=%async_computation.1 | async-start | bytes 2097152 | tf_op jit(solution)/shard_map/all_to_all | solution.py:414
  23.5 2.4 %collective-permute-start.4 = (bf16[384,768]{1,0:T(8,128)(2,1)}, bf16[384,768]{1,0:T(8,128)(2,1)}, u32[]{:S(2)}, u32[]{:S(2)}) collective-permute-start(bf16[384,768]{1,0:T(8,128)(2,1)} %bitcast.22), channel_id=1, source_target_pairs={{0,4},{1,5},{2,6},{3,7},{4,0},{5,1},{6,2},{7,3},{8,12},{9,13},{10,... | collective-permute-start | bytes 1769480 | tf_op jit(solution)/shard_map/ppermute | solution.py:404
  26.0 1.8 %collective-permute-start.5 = (bf16[384,768]{1,0:T(8,128)(2,1)}, bf16[384,768]{1,0:T(8,128)(2,1)}, u32[]{:S(2)}, u32[]{:S(2)}) collective-permute-start(bf16[384,768]{1,0:T(8,128)(2,1)} %bitcast.23), channel_id=1, source_target_pairs={{0,1},{1,0},{2,3},{3,2},{4,5},{5,4},{6,7},{7,6},{8,9},{9,8},{10,11... | collective-permute-start | bytes 1769480 | tf_op jit(solution)/shard_map/ppermute | solution.py:407
  28.4 8.0 %atom_attention.1 = (bf16[16,128,128]{2,1,0:T(8,128)(2,1)}, f32[8,128]{1,0:T(8,128)S(1)}) custom-call(s32[4]{0:T(128)S(1)} %copy-done.12, s32[1]{0:T(128)} %bitcast.3.off_ref, f32[16,4]{1,0:T(8,128)S(1)} %copy.26.wpair_ref, bf16[16,128,128]{2,1,0:T(8,128)(2,1)S(1)} %copy-done.8, bf16[16,128,128]{2,1,0:T(8,128)(2,1)S(1)} %collective-permute-done.before_ref, ...), custom_call_target="tpu_custom_call" | custom-call | flops 8000000000 | bytes 3000000 | tf_op jit(solution)/shard_map/atom_attention/pallas_call | solution.py:112
  37.0 2.3 %split_rows.1 = (bf16[1024,256]{1,0:T(8,128)(2,1)}, bf16[1024,256]{1,0:T(8,128)(2,1)}) custom-call(bf16[2048,256]{1,0:T(8,128)(2,1)} %bitcast.12.value_ref, f32[8,128]{1,0:T(8,128)} %copy-done.5), custom_call_target="tpu_custom_call" | custom-call | bytes 2097152 | tf_op jit(solution)/shard_map/split_rows/pallas_call | solution.py:154
  39.3 4.6 %collective-permute-start.7 = (bf16[384,768]{1,0:T(8,128)(2,1)}, bf16[384,768]{1,0:T(8,128)(2,1)S(1)}, u32[]{:S(2)}, u32[]{:S(2)}) collective-permute-start(bf16[384,768]{1,0:T(8,128)(2,1)} %tie.1.refs_2_), channel_id=1, source_target_pairs={{0,1},{1,0},{2,3},{3,2},{4,5},{5,4},{6,7},{7,6},{8,9},{9,8},{10,11... | collective-permute-start | bytes 1769480 | tf_op jit(solution)/shard_map/ppermute | solution.py:407
  43.9 4.6 %collective-permute-start.9 = (bf16[1024,256]{1,0:T(8,128)(2,1)}, bf16[1024,256]{1,0:T(8,128)(2,1)S(1)}, u32[]{:S(2)}, u32[]{:S(2)}) collective-permute-start(bf16[1024,256]{1,0:T(8,128)(2,1)} %get-tuple-element.15.refs_8_), channel_id=1, source_target_pairs={{0,6},{1,7},{2,0},{3,1},{4,2},{5,3},{6,4},{7,5},{8,14},{9,15},{10,... | collective-permute-start | bytes 1572872 | tf_op jit(solution)/shard_map/ppermute | solution.py:404
  48.5 3.7 %all-to-all-start = ((bf16[8,2,128,128]{3,2,1,0:T(8,128)(2,1)}), bf16[8,2,128,128]{3,2,1,0:T(8,128)(2,1)S(1)}, u32[]{:S(2)}, u32[]{:S(2)}) async-start(bf16[8,2,128,128]{3,2,1,0:T(8,128)(2,1)} %bitcast.8), calls=%async_computation | async-start | bytes 1048576 | tf_op jit(solution)/shard_map/all_to_all | solution.py:423
  54.7 1.4 collective-permute-start.10
  56.1 1.3 collective-permute-start.12
  57.5 8.1 %all-to-all-done.mid_ref = bf16[8,2,128,128]{3,2,1,0:T(8,128)(2,1)S(1)} async-done(((bf16[8,2,128,128]{3,2,1,0:T(8,128)(2,1)}), bf16[8,2,128,128]{3,2,1,0:T(8,128)(2,1)S(1)}, u32[]{:S(2)}, u32[]{:S(2)}) %all-to-all-start) | async-done | bytes 524320 | tf_op jit(solution)/shard_map/all_to_all | solution.py:423
  66.9 6.4 %pool_and_project.1 = (bf16[16,2,3,48,128]{4,3,2,1,0:T(8,128)(2,1)}, bf16[16,2,48,128]{3,2,1,0:T(8,128)(2,1)}, f32[2,128,768]{2,1,0:T(8,128)}) custom-call(s32[2]{0:T(128)} %pad_add_fusion.place_ref, bf16[8,2,128,128]{3,2,1,0:T(8,128)(2,1)} %copy-done.15, f32[1,128]{1,0:T(1,128)} %get-tuple-element.20.count_row_ref, f32[128,1]{1,0:T(8,128)} %copy.28.count_col_ref, ...), custom_call_target="tpu_custom_call" | custom-call | flops 6000000000 | bytes 8000000 | tf_op jit(solution)/shard_map/pool_and_project/pallas_call | solution.py:234
  73.3 4.6 %all-to-all-start.2 = ((bf16[16,2,3,48,128]{4,3,2,1,0:T(8,128)(2,1)}), bf16[16,2,3,48,128]{4,3,2,1,0:T(8,128)(2,1)}, u32[]{:S(2)}, u32[]{:S(2)}) async-start(bf16[16,2,3,48,128]{4,3,2,1,0:T(8,128)(2,1)} %get-tuple-element.16), calls=%async_computation.2 | async-start | bytes 2359296 | tf_op jit(solution)/shard_map/all_to_all | solution.py:437
  77.9 1.4 collective-permute-start.13
  79.4 1.0 collective-permute-start.11
  80.4 2.3 %collective-permute-start.18 = (bf16[1024,256]{1,0:T(8,128)(2,1)}, bf16[1024,256]{1,0:T(8,128)(2,1)S(1)}, u32[]{:S(2)}, u32[]{:S(2)}) collective-permute-start(bf16[1024,256]{1,0:T(8,128)(2,1)} %copy-done.19), channel_id=1, source_target_pairs={{0,6},{1,7},{2,0},{3,1},{4,2},{5,3},{6,4},{7,5},{8,14},{9,15},{10,... | collective-permute-start | bytes 1572872 | tf_op jit(solution)/shard_map/ppermute | solution.py:404
  82.8 1.4 collective-permute-done.17.refs_9_
  84.2 0.9 collective-permute-start.14
  86.4 9.1 %collective-permute-done.11.refs_2_ = bf16[1024,256]{1,0:T(8,128)(2,1)S(1)} collective-permute-done((bf16[1024,256]{1,0:T(8,128)(2,1)}, bf16[1024,256]{1,0:T(8,128)(2,1)S(1)}, u32[]{:S(2)}, u32[]{:S(2)}) %collective-permute-start.11) | collective-permute-done | bytes 524320 | tf_op jit(solution)/shard_map/ppermute | solution.py:404
  96.9 0.8 collective-permute-done.20.refs_13_
  98.6 0.8 copy-done.27
  99.4 15.6 %token_attention.1 = bf16[16,2,48,128]{3,2,1,0:T(8,128)(2,1)} custom-call(s32[2]{0:T(128)} %pad_add_fusion.place_ref, bf16[16,2,3,48,128]{4,3,2,1,0:T(8,128)(2,1)} %all-to-all-done.2.qkv_ref, bf16[1024,256]{1,0:T(8,128)(2,1)} %get-tuple-element.14.after_ref.refs_0_, bf16[1024,256]{1,0:T(8,128)(2,1)} %collective-permute-done.10.refs_1_, ...), custom_call_target="tpu_custom_call" | custom-call | flops 4294967296 | bytes 9568256 | tf_op jit(solution)/shard_map/token_attention/pallas_call | solution.py:316
  115.0 6.6 %all-to-all-start.3 = ((bf16[16,2,48,128]{3,2,1,0:T(8,128)(2,1)}), bf16[16,2,48,128]{3,2,1,0:T(8,128)(2,1)S(1)}, u32[]{:S(2)}, u32[]{:S(2)}) async-start(bf16[16,2,48,128]{3,2,1,0:T(8,128)(2,1)} %token_attention.1), calls=%async_computation.3 | async-start | bytes 786432 | tf_op jit(solution)/shard_map/all_to_all | solution.py:441
  121.8 9.1 %all-to-all-done.3.mixed_ref = bf16[16,2,48,128]{3,2,1,0:T(8,128)(2,1)S(1)} async-done(((bf16[16,2,48,128]{3,2,1,0:T(8,128)(2,1)}), bf16[16,2,48,128]{3,2,1,0:T(8,128)(2,1)S(1)}, u32[]{:S(2)}, u32[]{:S(2)}) %all-to-all-start.3) | async-done | bytes 393248 | tf_op jit(solution)/shard_map/all_to_all | solution.py:441
  131.7 14.5 %all_gather.3.back_ref = bf16[16,128,128]{2,1,0:T(8,128)(2,1)S(1)} all-gather(bf16[2,128,128]{2,1,0:T(8,128)(2,1)S(1)} %out_project.1), channel_id=1, replica_groups=mesh['seq'=16,'col'=8] {'col'}, dimensions={0}, use_global_device_ids=true | all-gather | bytes 589824 | tf_op jit(solution)/shard_map/all_gather | solution.py:443
  146.2 2.2 %spread_back.1 = bf16[16,128,128]{2,1,0:T(8,128)(2,1)} custom-call(s32[128,1]{1,0:T(8,128)S(1)} %copy.29.tok_ref, bf16[16,128,128]{2,1,0:T(8,128)(2,1)S(1)} %all_gather.3.back_ref, bf16[16,128,128]{2,1,0:T(8,128)(2,1)} %get-tuple-element.12.mid_ref), custom_call_target="tpu_custom_call" | custom-call | flops 100000000 | bytes 2000000 | tf_op jit(solution)/shard_map/spread_back/pallas_call | solution.py:369
  (99 shorter events, 9.6 us)
Async XLA Ops:
  0.0 27.8 %collective-permute-start.2 = (bf16[384,768]{1,0:T(8,128)(2,1)}, bf16[384,768]{1,0:T(8,128)(2,1)S(1)}, u32[]{:S(2)}, u32[]{:S(2)}) collective-permute-start(bf16[384,768]{1,0:T(8,128)(2,1)} %bitcast.20), channel_id=1, source_target_pairs={{0,2},{1,3},{2,4},{3,5},{4,6},{5,7},{6,0},{7,1},{8,10},{9,11},{10,... | collective-permute-start | bytes 1769480 | tf_op jit(solution)/shard_map/ppermute | solution.py:404
  2.0 25.9 %collective-permute-start.3 = (bf16[384,768]{1,0:T(8,128)(2,1)}, bf16[384,768]{1,0:T(8,128)(2,1)S(1)}, u32[]{:S(2)}, u32[]{:S(2)}) collective-permute-start(bf16[384,768]{1,0:T(8,128)(2,1)} %bitcast.21), channel_id=1, source_target_pairs={{0,6},{1,7},{2,0},{3,1},{4,2},{5,3},{6,4},{7,5},{8,14},{9,15},{10,... | collective-permute-start | bytes 1769480 | tf_op jit(solution)/shard_map/ppermute | solution.py:404
  3.4 22.6 %collective-permute-start = (bf16[16,128,128]{2,1,0:T(8,128)(2,1)}, bf16[16,128,128]{2,1,0:T(8,128)(2,1)S(1)}, u32[]{:S(2)}, u32[]{:S(2)}) collective-permute-start(bf16[16,128,128]{2,1,0:T(8,128)(2,1)} %feats_ref.1), channel_id=1, source_target_pairs={{0,1},{1,2},{2,3},{3,4},{4,5},{5,6},{6,7},{7,8},{8,9},{9,10},{10,1... | collective-permute-start | bytes 1572872 | tf_op jit(solution)/shard_map/ppermute | solution.py:395
  6.5 21.8 %collective-permute-start.1 = (bf16[16,128,128]{2,1,0:T(8,128)(2,1)}, bf16[16,128,128]{2,1,0:T(8,128)(2,1)S(1)}, u32[]{:S(2)}, u32[]{:S(2)}) collective-permute-start(bf16[16,128,128]{2,1,0:T(8,128)(2,1)} %feats_ref.1), channel_id=1, source_target_pairs={{1,0},{2,1},{3,2},{4,3},{5,4},{6,5},{7,6},{8,7},{9,8},{10,9},{11,1... | collective-permute-start | bytes 1572872 | tf_op jit(solution)/shard_map/ppermute | solution.py:396
  15.6 21.5 %all-to-all-start.1 = ((bf16[16,128,256]{2,1,0:T(8,128)(2,1)}), bf16[16,128,256]{2,1,0:T(8,128)(2,1)}, u32[]{:S(2)}, u32[]{:S(2)}) async-start(bf16[16,128,256]{2,1,0:T(8,128)(2,1)} %copy.27), calls=%async_computation.1 | async-start | bytes 2097152 | tf_op jit(solution)/shard_map/all_to_all | solution.py:414
  23.5 15.8 %collective-permute-start.4 = (bf16[384,768]{1,0:T(8,128)(2,1)}, bf16[384,768]{1,0:T(8,128)(2,1)}, u32[]{:S(2)}, u32[]{:S(2)}) collective-permute-start(bf16[384,768]{1,0:T(8,128)(2,1)} %bitcast.22), channel_id=1, source_target_pairs={{0,4},{1,5},{2,6},{3,7},{4,0},{5,1},{6,2},{7,3},{8,12},{9,13},{10,... | collective-permute-start | bytes 1769480 | tf_op jit(solution)/shard_map/ppermute | solution.py:404
  26.0 28.7 %collective-permute-start.5 = (bf16[384,768]{1,0:T(8,128)(2,1)}, bf16[384,768]{1,0:T(8,128)(2,1)}, u32[]{:S(2)}, u32[]{:S(2)}) collective-permute-start(bf16[384,768]{1,0:T(8,128)(2,1)} %bitcast.23), channel_id=1, source_target_pairs={{0,1},{1,0},{2,3},{3,2},{4,5},{5,4},{6,7},{7,6},{8,9},{9,8},{10,11... | collective-permute-start | bytes 1769480 | tf_op jit(solution)/shard_map/ppermute | solution.py:407
  27.9 28.2 %collective-permute-start.6 = (bf16[384,768]{1,0:T(8,128)(2,1)S(1)}, bf16[384,768]{1,0:T(8,128)(2,1)}, u32[]{:S(2)}, u32[]{:S(2)}) collective-permute-start(bf16[384,768]{1,0:T(8,128)(2,1)S(1)} %collective-permute-done.2.refs_0_.refs_1_), channel_id=1, source_target_pairs={{0,1},{1,0},{2,3},{3,2},{4,5},{5,4},{6,7},{7,6},{8,9},{9,8},{10,11... | collective-permute-start | bytes 1769480 | tf_op jit(solution)/shard_map/ppermute | solution.py:407
  28.0 29.4 %collective-permute-start.8 = (bf16[384,768]{1,0:T(8,128)(2,1)S(1)}, bf16[384,768]{1,0:T(8,128)(2,1)}, u32[]{:S(2)}, u32[]{:S(2)}) collective-permute-start(bf16[384,768]{1,0:T(8,128)(2,1)S(1)} %collective-permute-done.3.refs_1_.refs_3_), channel_id=1, source_target_pairs={{0,1},{1,0},{2,3},{3,2},{4,5},{5,4},{6,7},{7,6},{8,9},{9,8},{10,11... | collective-permute-start | bytes 1769480 | tf_op jit(solution)/shard_map/ppermute | solution.py:407
  39.3 26.4 %collective-permute-start.7 = (bf16[384,768]{1,0:T(8,128)(2,1)}, bf16[384,768]{1,0:T(8,128)(2,1)S(1)}, u32[]{:S(2)}, u32[]{:S(2)}) collective-permute-start(bf16[384,768]{1,0:T(8,128)(2,1)} %tie.1.refs_2_), channel_id=1, source_target_pairs={{0,1},{1,0},{2,3},{3,2},{4,5},{5,4},{6,7},{7,6},{8,9},{9,8},{10,11... | collective-permute-start | bytes 1769480 | tf_op jit(solution)/shard_map/ppermute | solution.py:407
  43.9 21.8 %collective-permute-start.9 = (bf16[1024,256]{1,0:T(8,128)(2,1)}, bf16[1024,256]{1,0:T(8,128)(2,1)S(1)}, u32[]{:S(2)}, u32[]{:S(2)}) collective-permute-start(bf16[1024,256]{1,0:T(8,128)(2,1)} %get-tuple-element.15.refs_8_), channel_id=1, source_target_pairs={{0,6},{1,7},{2,0},{3,1},{4,2},{5,3},{6,4},{7,5},{8,14},{9,15},{10,... | collective-permute-start | bytes 1572872 | tf_op jit(solution)/shard_map/ppermute | solution.py:404
  48.5 17.2 %all-to-all-start = ((bf16[8,2,128,128]{3,2,1,0:T(8,128)(2,1)}), bf16[8,2,128,128]{3,2,1,0:T(8,128)(2,1)S(1)}, u32[]{:S(2)}, u32[]{:S(2)}) async-start(bf16[8,2,128,128]{3,2,1,0:T(8,128)(2,1)} %bitcast.8), calls=%async_computation | async-start | bytes 1048576 | tf_op jit(solution)/shard_map/all_to_all | solution.py:423
  54.7 24.7 %collective-permute-start.10 = (bf16[1024,256]{1,0:T(8,128)(2,1)S(1)}, bf16[1024,256]{1,0:T(8,128)(2,1)}, u32[]{:S(2)}, u32[]{:S(2)}) collective-permute-start(bf16[1024,256]{1,0:T(8,128)(2,1)S(1)} %copy-done.14), channel_id=1, source_target_pairs={{0,2},{1,3},{2,4},{3,5},{4,6},{5,7},{6,0},{7,1},{8,10},{9,11},{10,... | collective-permute-start | bytes 1572872 | tf_op jit(solution)/shard_map/ppermute | solution.py:404
  56.1 24.4 %collective-permute-start.12 = (bf16[1024,256]{1,0:T(8,128)(2,1)S(1)}, bf16[1024,256]{1,0:T(8,128)(2,1)}, u32[]{:S(2)}, u32[]{:S(2)}) collective-permute-start(bf16[1024,256]{1,0:T(8,128)(2,1)S(1)} %copy-done.14), channel_id=1, source_target_pairs={{0,6},{1,7},{2,0},{3,1},{4,2},{5,3},{6,4},{7,5},{8,14},{9,15},{10,... | collective-permute-start | bytes 1572872 | tf_op jit(solution)/shard_map/ppermute | solution.py:404
  57.4 26.8 %collective-permute-start.17 = (bf16[1024,256]{1,0:T(8,128)(2,1)}, bf16[1024,256]{1,0:T(8,128)(2,1)}, u32[]{:S(2)}, u32[]{:S(2)}) collective-permute-start(bf16[1024,256]{1,0:T(8,128)(2,1)} %get-tuple-element.15.refs_8_), channel_id=1, source_target_pairs={{0,2},{1,3},{2,4},{3,5},{4,6},{5,7},{6,0},{7,1},{8,10},{9,11},{10,... | collective-permute-start | bytes 1572872 | tf_op jit(solution)/shard_map/ppermute | solution.py:404
  73.3 26.2 %all-to-all-start.2 = ((bf16[16,2,3,48,128]{4,3,2,1,0:T(8,128)(2,1)}), bf16[16,2,3,48,128]{4,3,2,1,0:T(8,128)(2,1)}, u32[]{:S(2)}, u32[]{:S(2)}) async-start(bf16[16,2,3,48,128]{4,3,2,1,0:T(8,128)(2,1)} %get-tuple-element.16), calls=%async_computation.2 | async-start | bytes 2359296 | tf_op jit(solution)/shard_map/all_to_all | solution.py:437
  77.9 43.8 %copy-start.29 = (s32[128]{0:T(128)S(1)}, s32[128]{0:T(128)}, u32[]{:S(2)}) copy-start(s32[128]{0:T(128)} %param.19) | copy-start | bytes 1540
  77.9 53.0 %copy-start.1 = (bf16[768,768]{1,0:T(8,128)(2,1)S(1)}, bf16[768,768]{1,0:T(8,128)(2,1)}, u32[]{:S(2)}) copy-start(bf16[768,768]{1,0:T(8,128)(2,1)} %out_proj_ref.3) | copy-start | bytes 3538948
  77.9 53.0 %copy-start.2 = (f32[2,128,768]{2,1,0:T(8,128)S(1)}, f32[2,128,768]{2,1,0:T(8,128)}, u32[]{:S(2)}) copy-start(f32[2,128,768]{2,1,0:T(8,128)} %get-tuple-element.18.single_ref) | copy-start | bytes 2359300
  77.9 53.0 %copy-start.3 = (bf16[16,2,48,128]{3,2,1,0:T(8,128)(2,1)S(1)}, bf16[16,2,48,128]{3,2,1,0:T(8,128)(2,1)}, u32[]{:S(2)}) copy-start(bf16[16,2,48,128]{3,2,1,0:T(8,128)(2,1)} %get-tuple-element.17.gate_ref) | copy-start | bytes 1179652
  77.9 53.0 %copy-start.4 = (bf16[768,128]{1,0:T(8,128)(2,1)S(1)}, bf16[768,128]{1,0:T(8,128)(2,1)}, u32[]{:S(2)}) copy-start(bf16[768,128]{1,0:T(8,128)(2,1)} %return_ref.1) | copy-start | bytes 589828
  77.9 7.1 %collective-permute-start.13 = (bf16[1024,256]{1,0:T(8,128)(2,1)S(1)}, bf16[1024,256]{1,0:T(8,128)(2,1)S(1)}, u32[]{:S(2)}, u32[]{:S(2)}) collective-permute-start(bf16[1024,256]{1,0:T(8,128)(2,1)S(1)} %copy-done.14), channel_id=1, source_target_pairs={{0,1},{1,0},{2,3},{3,2},{4,5},{5,4},{6,7},{7,6},{8,9},{9,8},{10,11... | collective-permute-start | bytes 1572872 | tf_op jit(solution)/shard_map/ppermute | solution.py:407
  79.3 6.5 %collective-permute-start.19 = (bf16[1024,256]{1,0:T(8,128)(2,1)}, bf16[1024,256]{1,0:T(8,128)(2,1)}, u32[]{:S(2)}, u32[]{:S(2)}) collective-permute-start(bf16[1024,256]{1,0:T(8,128)(2,1)} %get-tuple-element.15.refs_8_), channel_id=1, source_target_pairs={{0,1},{1,0},{2,3},{3,2},{4,5},{5,4},{6,7},{7,6},{8,9},{9,8},{10,11... | collective-permute-start | bytes 1572872 | tf_op jit(solution)/shard_map/ppermute | solution.py:407
  79.4 16.0 %collective-permute-start.11 = (bf16[1024,256]{1,0:T(8,128)(2,1)}, bf16[1024,256]{1,0:T(8,128)(2,1)S(1)}, u32[]{:S(2)}, u32[]{:S(2)}) collective-permute-start(bf16[1024,256]{1,0:T(8,128)(2,1)} %collective-permute-done.10.refs_1_), channel_id=1, source_target_pairs={{0,2},{1,3},{2,4},{3,5},{4,6},{5,7},{6,0},{7,1},{8,10},{9,11},{10,... | collective-permute-start | bytes 1572872 | tf_op jit(solution)/shard_map/ppermute | solution.py:404
  80.4 15.6 %collective-permute-start.18 = (bf16[1024,256]{1,0:T(8,128)(2,1)}, bf16[1024,256]{1,0:T(8,128)(2,1)S(1)}, u32[]{:S(2)}, u32[]{:S(2)}) collective-permute-start(bf16[1024,256]{1,0:T(8,128)(2,1)} %copy-done.19), channel_id=1, source_target_pairs={{0,6},{1,7},{2,0},{3,1},{4,2},{5,3},{6,4},{7,5},{8,14},{9,15},{10,... | collective-permute-start | bytes 1572872 | tf_op jit(solution)/shard_map/ppermute | solution.py:404
  84.2 12.6 %collective-permute-start.14 = (bf16[1024,256]{1,0:T(8,128)(2,1)}, bf16[1024,256]{1,0:T(8,128)(2,1)S(1)}, u32[]{:S(2)}, u32[]{:S(2)}) collective-permute-start(bf16[1024,256]{1,0:T(8,128)(2,1)} %collective-permute-done.10.refs_1_), channel_id=1, source_target_pairs={{0,1},{1,0},{2,3},{3,2},{4,5},{5,4},{6,7},{7,6},{8,9},{9,8},{10,11... | collective-permute-start | bytes 1572872 | tf_op jit(solution)/shard_map/ppermute | solution.py:407
  85.8 11.1 %collective-permute-start.22 = (bf16[1024,256]{1,0:T(8,128)(2,1)}, bf16[1024,256]{1,0:T(8,128)(2,1)S(1)}, u32[]{:S(2)}, u32[]{:S(2)}) collective-permute-start(bf16[1024,256]{1,0:T(8,128)(2,1)} %copy-done.19), channel_id=1, source_target_pairs={{0,1},{1,0},{2,3},{3,2},{4,5},{5,4},{6,7},{7,6},{8,9},{9,8},{10,11... | collective-permute-start | bytes 1572872 | tf_op jit(solution)/shard_map/ppermute | solution.py:407
  85.9 11.1 %collective-permute-start.16 = (bf16[1024,256]{1,0:T(8,128)(2,1)}, bf16[1024,256]{1,0:T(8,128)(2,1)S(1)}, u32[]{:S(2)}, u32[]{:S(2)}) collective-permute-start(bf16[1024,256]{1,0:T(8,128)(2,1)} %collective-permute-done.12.refs_3_), channel_id=1, source_target_pairs={{0,1},{1,0},{2,3},{3,2},{4,5},{5,4},{6,7},{7,6},{8,9},{9,8},{10,11... | collective-permute-start | bytes 1572872 | tf_op jit(solution)/shard_map/ppermute | solution.py:407
  95.4 2.3 %collective-permute-start.20 = (bf16[1024,256]{1,0:T(8,128)(2,1)}, bf16[1024,256]{1,0:T(8,128)(2,1)S(1)}, u32[]{:S(2)}, u32[]{:S(2)}) collective-permute-start(bf16[1024,256]{1,0:T(8,128)(2,1)} %collective-permute-done.17.refs_9_), channel_id=1, source_target_pairs={{0,1},{1,0},{2,3},{3,2},{4,5},{5,4},{6,7},{7,6},{8,9},{9,8},{10,11... | collective-permute-start | bytes 1572872 | tf_op jit(solution)/shard_map/ppermute | solution.py:407
  96.2 2.1 %collective-permute-start.15 = (bf16[1024,256]{1,0:T(8,128)(2,1)S(1)}, bf16[1024,256]{1,0:T(8,128)(2,1)S(1)}, u32[]{:S(2)}, u32[]{:S(2)}) collective-permute-start(bf16[1024,256]{1,0:T(8,128)(2,1)S(1)} %collective-permute-done.11.refs_2_), channel_id=1, source_target_pairs={{0,1},{1,0},{2,3},{3,2},{4,5},{5,4},{6,7},{7,6},{8,9},{9,8},{10,11... | collective-permute-start | bytes 1572872 | tf_op jit(solution)/shard_map/ppermute | solution.py:407
  96.8 2.6 %collective-permute-start.21 = (bf16[1024,256]{1,0:T(8,128)(2,1)S(1)}, bf16[1024,256]{1,0:T(8,128)(2,1)}, u32[]{:S(2)}, u32[]{:S(2)}) collective-permute-start(bf16[1024,256]{1,0:T(8,128)(2,1)S(1)} %collective-permute-done.18.refs_10_), channel_id=1, source_target_pairs={{0,1},{1,0},{2,3},{3,2},{4,5},{5,4},{6,7},{7,6},{8,9},{9,8},{10,11... | collective-permute-start | bytes 1572872 | tf_op jit(solution)/shard_map/ppermute | solution.py:407
  115.0 15.8 %all-to-all-start.3 = ((bf16[16,2,48,128]{3,2,1,0:T(8,128)(2,1)}), bf16[16,2,48,128]{3,2,1,0:T(8,128)(2,1)S(1)}, u32[]{:S(2)}, u32[]{:S(2)}) async-start(bf16[16,2,48,128]{3,2,1,0:T(8,128)(2,1)} %token_attention.1), calls=%async_computation.3 | async-start | bytes 786432 | tf_op jit(solution)/shard_map/all_to_all | solution.py:441
  (25 other events, 183.9 us)
